TPU v7x, 512 devices: a whole 4x8x8 slice. The times are simulated.
512 devices in a mesh: seg: 16 (over x, z_lo), space: 32 (over z_hi, y, core).
Axes of the slice: x: 4, y: 8, z: 8 (z_hi: 2, z_lo: 4; z = z_hi * 4 + z_lo), core: 2. Of those that a mesh axis runs over, the one named last changes fastest.
Arguments:
- basis: bfloat16 [16, 8, 1024, 1024], P('seg', None, 'space'), may hold values from -16 to 16
- base_grad: bfloat16 [16, 2, 2, 1024, 1024], P('seg', None, None, 'space'), may hold values from -8 to 8
- step_counts: int32 [16], P('seg'), may hold values from 2 to 8
- shift: int32 [2], replicated, may hold values from 0 to 1023
Outputs:
- new_vector: float32 [16, 1024, 1024], P('seg', 'space')
- hessenberg: float32 [9], replicated
All inputs are finite; a program needn't handle non-finite values.
Results may differ from a plain program's by a relative error of at most 0.0003.
Values may be sent and summed in bfloat16 or wider, within the bound.
A program may use at most 64 MiB of HBM per device.

v0:
```python
import math

import jax
import jax.numpy as jnp
from jax import lax
from jax.sharding import PartitionSpec as P

highest = lax.Precision.HIGHEST


def passed_along(value, axis, steps):
    count = lax.axis_size(axis)
    pairs = [(source, (source + steps) % count) for source in range(count)]
    return lax.ppermute(value, axis, pairs)


def phi_pair(scaled):
    small = jnp.abs(scaled) < 0.5
    safe = jnp.where(small, jnp.ones_like(scaled), scaled)
    growth = jnp.expm1(safe)
    first_phi = growth / safe
    second_phi = (growth - safe) / (safe * safe)
    series_one = jnp.zeros_like(scaled)
    series_two = jnp.zeros_like(scaled)
    for power in range(10, -1, -1):
        fact_one = 1.0
        for factor in range(2, power + 2):
            fact_one = fact_one * factor
        fact_two = fact_one * (power + 2)
        series_one = series_one * scaled + 1.0 / fact_one
        series_two = series_two * scaled + 1.0 / fact_two
    return (
        jnp.exp(scaled),
        jnp.where(small, series_one, first_phi),
        jnp.where(small, series_two, second_phi),
    )


def unit_roots(size_first, size_second, period, direction):
    first_index = jnp.arange(size_first, dtype=jnp.int32)[:, None]
    second_index = jnp.arange(size_second, dtype=jnp.int32)[None, :]
    angles = 2.0 * math.pi / period * (first_index * second_index % period).astype(jnp.float32)
    return (jnp.cos(angles), direction * jnp.sin(angles))


def complex_contract(form, real_in, imag_in, table_real, table_imag):

    def product(operand, factor):
        return jnp.einsum(form, operand, factor, precision=highest)

    if imag_in is None:
        return (product(real_in, table_real), product(real_in, table_imag))
    return (
        product(real_in, table_real) - product(imag_in, table_imag),
        product(real_in, table_imag) + product(imag_in, table_real),
    )


def rotate(packed):
    half_width = packed.shape[-1] // 2
    return jnp.concatenate([-packed[..., half_width:], packed[..., :half_width]], axis=-1)


def packed_contract(form, packed, table_real, table_imag):
    return jnp.einsum(form, packed, table_real, precision=highest) + jnp.einsum(
        form, rotate(packed), table_imag, precision=highest
    )


def rows_forward(real_in):
    row_count, length = real_in.shape
    inner_len = length // 16
    shaped_real = real_in.reshape(row_count, 16, inner_len)
    shaped_imag = None
    short_real, short_imag = unit_roots(16, 16, 16, -1.0)
    real_mid, imag_mid = complex_contract(
        "rnq,nk->rkq", shaped_real, shaped_imag, short_real, short_imag
    )
    twist_real, twist_imag = unit_roots(16, inner_len, length, -1.0)
    real_mid, imag_mid = (
        real_mid * twist_real - imag_mid * twist_imag,
        real_mid * twist_imag + imag_mid * twist_real,
    )
    long_real, long_imag = unit_roots(inner_len, inner_len, inner_len, -1.0)
    real_out, imag_out = complex_contract("rkq,qm->rkm", real_mid, imag_mid, long_real, long_imag)
    return (real_out.reshape(row_count, length), imag_out.reshape(row_count, length))


def rows_inverse(real_in, imag_in):
    row_count, length = real_in.shape
    inner_len = length // 16
    shaped_real = real_in.reshape(row_count, 16, inner_len)
    shaped_imag = imag_in.reshape(row_count, 16, inner_len)
    long_real, long_imag = unit_roots(inner_len, inner_len, inner_len, 1.0)
    real_mid, imag_mid = complex_contract(
        "rkm,mq->rkq", shaped_real, shaped_imag, long_real, long_imag
    )
    twist_real, twist_imag = unit_roots(16, inner_len, length, 1.0)
    real_mid, imag_mid = (
        real_mid * twist_real - imag_mid * twist_imag,
        real_mid * twist_imag + imag_mid * twist_real,
    )
    short_real, short_imag = unit_roots(16, 16, 16, 1.0)
    real_out, imag_out = complex_contract("rkq,kn->rnq", real_mid, imag_mid, short_real, short_imag)
    return (real_out.reshape(row_count, length), imag_out.reshape(row_count, length))


def columns_forward(packed):
    length, width = packed.shape
    inner_len = length // 16
    shaped = packed.reshape(16, inner_len, width)
    short_real, short_imag = unit_roots(16, 16, 16, -1.0)
    shaped = packed_contract("nqc,nk->kqc", shaped, short_real, short_imag)
    twist_real, twist_imag = unit_roots(16, inner_len, length, -1.0)
    shaped = twist_real[:, :, None] * shaped + twist_imag[:, :, None] * rotate(shaped)
    long_real, long_imag = unit_roots(inner_len, inner_len, inner_len, -1.0)
    shaped = packed_contract("kqc,qm->kmc", shaped, long_real, long_imag)
    return shaped.reshape(length, width)


def columns_inverse(packed):
    length, width = packed.shape
    inner_len = length // 16
    shaped = packed.reshape(16, inner_len, width)
    long_real, long_imag = unit_roots(inner_len, inner_len, inner_len, 1.0)
    shaped = packed_contract("kmc,mq->kqc", shaped, long_real, long_imag)
    twist_real, twist_imag = unit_roots(16, inner_len, length, 1.0)
    shaped = twist_real[:, :, None] * shaped + twist_imag[:, :, None] * rotate(shaped)
    short_real, short_imag = unit_roots(16, 16, 16, 1.0)
    shaped = packed_contract("kqc,kn->nqc", shaped, short_real, short_imag)
    return shaped.reshape(length, width)


def forward_field(values):
    real_part, imag_part = rows_forward(values)
    stacked = jnp.stack([real_part, imag_part], axis=1)
    moved = lax.all_to_all(stacked, "space", split_axis=2, concat_axis=0, tiled=True)
    return columns_forward(moved.reshape(moved.shape[0], -1))


def inverse_field(packed):
    length = packed.shape[0]
    spread = columns_inverse(packed).reshape(length, 2, -1)
    moved = lax.all_to_all(spread, "space", split_axis=0, concat_axis=2, tiled=True)
    real_part, imag_part = rows_inverse(moved[:, 0], moved[:, 1])
    factor = 1.0 / (length * length)
    return (real_part * factor, imag_part * factor)


def signed_scrambled(index, length):
    inner_len = length // 16
    freq = index // inner_len + 16 * (index % inner_len)
    return jnp.where(freq < length // 2, freq, freq - length)


def per_device(basis, base_grad, step_counts, shift):
    vectors = basis[0]
    grads = base_grad[0]
    start = vectors[-1].astype(jnp.float32)
    length = vectors.shape[2]
    space_count = lax.axis_size("space")
    space_index = lax.axis_index("space")
    row_freq = signed_scrambled(jnp.arange(length, dtype=jnp.int32), length)
    local_cols = length // space_count
    col_freq = signed_scrambled(
        space_index * local_cols + jnp.arange(local_cols, dtype=jnp.int32), length
    )
    col_freq = jnp.concatenate([col_freq, col_freq])
    wave_x = (row_freq.astype(jnp.float32) * (8.0 / length))[:, None]
    wave_y = (col_freq.astype(jnp.float32) * (8.0 / length))[None, :]
    deriv_x = jnp.where(row_freq[:, None] == -(length // 2), jnp.zeros_like(wave_x), wave_x)
    deriv_y = jnp.where(col_freq[None, :] == -(length // 2), jnp.zeros_like(wave_y), wave_y)
    squared = wave_x * wave_x + wave_y * wave_y
    linear = squared - squared * squared
    step_size = 0.01 * step_counts[0].astype(jnp.float32)
    decay, phi_one, phi_two = phi_pair(linear * step_size)
    side_wave = wave_x[:, 0] * wave_x[:, 0] + 16.0
    side_linear = side_wave - side_wave * side_wave
    decay_side, phi_one_side, phi_two_side = phi_pair(side_linear * step_size)
    at_anchor = space_index == 0
    decay_side = jnp.where(at_anchor, decay_side, decay[:, 0])
    phi_one_side = jnp.where(at_anchor, phi_one_side, phi_one[:, 0])
    phi_two_side = jnp.where(at_anchor, phi_two_side, phi_two[:, 0])

    def scaled_by(full_mult, field):
        return full_mult * field

    def nonlinear(packed, section_index):
        grad_x, grad_y = inverse_field(deriv_x * rotate(packed) - deriv_y * packed)
        term = -(
            grads[section_index, 0].astype(jnp.float32) * grad_x
            + grads[section_index, 1].astype(jnp.float32) * grad_y
        )
        return forward_field(term)

    state = forward_field(start)
    section_index = 0
    now_term = nonlinear(state, section_index)
    middle = scaled_by(decay, state) + scaled_by(step_size * phi_one, now_term)
    state = middle + scaled_by(step_size * phi_two, nonlinear(middle, section_index + 1) - now_term)
    offsets = (row_freq[:, None] * shift[0] + col_freq[None, :] * shift[1]) % length
    angles = 2.0 * math.pi / length * offsets.astype(jnp.float32)
    is_last = lax.axis_index("seg") == lax.axis_size("seg") - 1
    cosine = jnp.where(is_last, jnp.cos(angles), jnp.ones_like(angles))
    sine = jnp.where(is_last, jnp.sin(angles), jnp.zeros_like(angles))
    phased = cosine * state - sine * rotate(state)
    flowed = inverse_field(phased)[0]
    cells = float(lax.axis_size("seg") * length * length)
    incoming = passed_along(flowed, "seg", 1)
    residual_in = incoming - start
    widened = vectors.astype(jnp.float32)
    local_dots = jnp.einsum("kxy,xy->k", widened, residual_in, precision=highest)
    coeffs = lax.psum(local_dots, ("seg", "space")) / cells
    remainder = residual_in - jnp.einsum("k,kxy->xy", coeffs, widened, precision=highest)
    norm_sq = lax.psum(jnp.sum(remainder * remainder), ("seg", "space")) / cells
    norm_value = jnp.sqrt(norm_sq)
    return ((remainder / norm_value)[None], jnp.concatenate([coeffs, norm_value[None]]))


def solution(mesh):
    in_specs = (P("seg", None, "space", None), P("seg", None, None, "space", None), P("seg"), P())
    out_specs = (P("seg", "space", None), P())
    return jax.shard_map(
        per_device, mesh=mesh, in_specs=in_specs, out_specs=out_specs, check_vma=False
    )
```

profile of v0, /device:TPU:1, one launch (start us, length us, event | category | flops | bytes accessed | tf_op | source)
XLA Modules:
  0.0 440.8 jit_solution(4325354481679966277)
XLA Ops:
  0.7 0.8 slice-done
  5.5 1.7 reshape.341
  7.3 17.4 %all-to-all-start = ((f32[32,1,2048]{2,1,0:T(1,128)}), f32[32,1,2048]{2,1,0:T(1,128)S(1)}, u32[]{:S(2)}, u32[]{:S(2)}) async-start(f32[32,1,2048]{2,1,0:T(1,128)} %reshape.341), calls=%async_computation | async-start | bytes 524288 | tf_op jit(solution)/shard_map/all_to_all | solution.py:137
  25.6 14.7 %all-to-all-done = f32[32,1,2048]{2,1,0:T(1,128)S(1)} async-done(((f32[32,1,2048]{2,1,0:T(1,128)}), f32[32,1,2048]{2,1,0:T(1,128)S(1)}, u32[]{:S(2)}, u32[]{:S(2)}) %all-to-all-start) | async-done | bytes 262176 | tf_op jit(solution)/shard_map/all_to_all | solution.py:137
  40.8 1.3 reduce
  42.1 0.9 reshape.342
  45.0 0.7 convolution_add_fusion.5
  47.4 0.7 fusion.164
  48.1 0.7 fusion.199
  50.0 0.7 fusion.222
  51.0 0.7 fusion.197
  53.6 1.1 convolution_add_fusion.4
  55.5 1.7 reshape.343
  57.2 5.1 %all-to-all-start.1 = ((f32[32,1,2048]{2,1,0:T(1,128)}), f32[32,1,2048]{2,1,0:T(1,128)S(1)}, u32[]{:S(2)}, u32[]{:S(2)}) async-start(f32[32,1,2048]{2,1,0:T(1,128)} %reshape.343), calls=%async_computation.1 | async-start | bytes 524288 | tf_op jit(solution)/shard_map/all_to_all | solution.py:144
  62.4 0.7 slice_convert_fusion.1
  63.1 0.8 reshape.300
  64.0 14.3 %all-to-all-done.1 = f32[32,1,2048]{2,1,0:T(1,128)S(1)} async-done(((f32[32,1,2048]{2,1,0:T(1,128)}), f32[32,1,2048]{2,1,0:T(1,128)S(1)}, u32[]{:S(2)}, u32[]{:S(2)}) %all-to-all-start.1) | async-done | bytes 262176 | tf_op jit(solution)/shard_map/all_to_all | solution.py:144
  78.3 1.3 reduce.1
  79.6 0.9 reshape.344
  90.5 1.7 reshape.345
  92.3 5.2 %all-to-all-start.2 = ((f32[32,1,2048]{2,1,0:T(1,128)}), f32[32,1,2048]{2,1,0:T(1,128)S(1)}, u32[]{:S(2)}, u32[]{:S(2)}) async-start(f32[32,1,2048]{2,1,0:T(1,128)} %reshape.345), calls=%async_computation.2 | async-start | bytes 524288 | tf_op jit(solution)/shard_map/all_to_all | solution.py:137
  98.1 15.1 %all-to-all-done.2 = f32[32,1,2048]{2,1,0:T(1,128)S(1)} async-done(((f32[32,1,2048]{2,1,0:T(1,128)}), f32[32,1,2048]{2,1,0:T(1,128)S(1)}, u32[]{:S(2)}, u32[]{:S(2)}) %all-to-all-start.2) | async-done | bytes 262176 | tf_op jit(solution)/shard_map/all_to_all | solution.py:137
  113.2 1.3 reduce.2
  114.5 0.9 reshape.346
  117.4 0.7 convolution_add_fusion.3
  119.7 0.7 fusion.162
  120.5 0.7 fusion.195
  123.9 0.9 fusion.46
  124.9 0.7 fusion.217
  125.9 0.7 fusion.201
  127.2 0.9 fusion.47
  128.9 0.7 convolution_add_fusion.2
  130.3 1.7 reshape.347
  132.1 5.1 %all-to-all-start.3 = ((f32[32,1,2048]{2,1,0:T(1,128)}), f32[32,1,2048]{2,1,0:T(1,128)S(1)}, u32[]{:S(2)}, u32[]{:S(2)}) async-start(f32[32,1,2048]{2,1,0:T(1,128)} %reshape.347), calls=%async_computation.3 | async-start | bytes 524288 | tf_op jit(solution)/shard_map/all_to_all | solution.py:144
  137.3 0.8 reshape.302
  138.2 0.8 reshape.301
  139.0 14.2 %all-to-all-done.3 = f32[32,1,2048]{2,1,0:T(1,128)S(1)} async-done(((f32[32,1,2048]{2,1,0:T(1,128)}), f32[32,1,2048]{2,1,0:T(1,128)S(1)}, u32[]{:S(2)}, u32[]{:S(2)}) %all-to-all-start.3) | async-done | bytes 262176 | tf_op jit(solution)/shard_map/all_to_all | solution.py:144
  153.2 1.3 reduce.3
  154.5 0.9 reshape.348
  165.8 1.7 reshape.349
  167.6 5.3 %all-to-all-start.4 = ((f32[32,1,2048]{2,1,0:T(1,128)}), f32[32,1,2048]{2,1,0:T(1,128)S(1)}, u32[]{:S(2)}, u32[]{:S(2)}) async-start(f32[32,1,2048]{2,1,0:T(1,128)} %reshape.349), calls=%async_computation.4 | async-start | bytes 524288 | tf_op jit(solution)/shard_map/all_to_all | solution.py:137
  175.3 0.7 broadcast_multiply_fusion.1
  176.0 12.7 %all-to-all-done.4 = f32[32,1,2048]{2,1,0:T(1,128)S(1)} async-done(((f32[32,1,2048]{2,1,0:T(1,128)}), f32[32,1,2048]{2,1,0:T(1,128)S(1)}, u32[]{:S(2)}, u32[]{:S(2)}) %all-to-all-start.4) | async-done | bytes 262176 | tf_op jit(solution)/shard_map/all_to_all | solution.py:137
  188.7 1.3 reduce.4
  190.0 0.9 reshape.350
  192.9 0.7 convolution_add_fusion.1
  195.2 0.7 fusion.166
  195.9 0.7 fusion.191
  197.2 0.8 copy-done.1
  198.9 3.9 fusion.32
  202.9 0.7 fusion.219
  203.8 0.7 fusion.193
  206.4 0.7 convolution_add_fusion
  207.9 1.0 reshape.351
  209.0 20.3 %all_to_all.99 = f32[32,1,2048]{2,1,0:T(1,128)S(1)} all-to-all(f32[32,1,2048]{2,1,0:T(1,128)S(1)} %reshape.351), channel_id=1, replica_groups=mesh['seg'=16,'space'=32] {'space'}, dimensions={0} | all-to-all | bytes 524288 | tf_op jit(solution)/shard_map/all_to_all | solution.py:144
  229.3 1.3 reduce.5
  230.6 0.9 reshape.352
  236.1 3.1 collective-permute-start
  239.1 6.5 %collective-permute-done = f32[32,1024]{1,0:T(8,128)S(1)} collective-permute-done((f32[32,1024]{1,0:T(8,128)S(1)}, f32[32,1024]{1,0:T(8,128)S(1)}, u32[]{:S(2)}, u32[]{:S(2)}) %collective-permute-start) | collective-permute-done | bytes 131104 | tf_op jit(solution)/shard_map/ppermute | solution.py:14
  245.7 1.5 convolution_bitcast_fusion
  247.2 95.1 %psum.14 = f32[8]{0:T(128)S(1)} all-reduce(f32[8]{0:T(128)S(1)} %convolution_bitcast_fusion), channel_id=1, replica_groups=mesh['seg'=16,'space'=32] {'seg','space'}, use_global_device_ids=true, to_apply=%region_0.1 | all-reduce | flops 8 | bytes 64 | tf_op jit(solution)/shard_map/psum | solution.py:213
  342.3 0.7 fusion.60
  343.7 94.8 %psum.15 = f32[]{:T(128)} all-reduce(f32[]{:T(128)} %multiply_reduce_fusion), channel_id=1, replica_groups=mesh['seg'=16,'space'=32] {'seg','space'}, use_global_device_ids=true, to_apply=%region_2.3 | all-reduce | flops 1 | bytes 8 | tf_op jit(solution)/shard_map/psum | solution.py:215
  439.8 0.7 divide_bitcast_fusion
  (212 shorter events, 58.3 us)
Async XLA Ops:
  0.7 0.8 slice-start
  7.3 33.0 %all-to-all-start = ((f32[32,1,2048]{2,1,0:T(1,128)}), f32[32,1,2048]{2,1,0:T(1,128)S(1)}, u32[]{:S(2)}, u32[]{:S(2)}) async-start(f32[32,1,2048]{2,1,0:T(1,128)} %reshape.341), calls=%async_computation | async-start | bytes 524288 | tf_op jit(solution)/shard_map/all_to_all | solution.py:137
  25.0 0.5 copy-start.12
  25.6 24.2 %copy-start.9 = (f32[64]{0:T(128)}, f32[64]{0:T(128)S(1)}, u32[]{:S(2)}) copy-start(f32[64]{0:T(128)S(1)} %get-tuple-element.69) | copy-start | bytes 772
  57.2 5.2 %copy-start.8 = (bf16[1,2,2,32,1024]{4,3,2,1,0:T(8,128)(2,1)S(1)}, bf16[1,2,2,32,1024]{4,3,2,1,0:T(8,128)(2,1)}, u32[]{:S(2)}) copy-start(bf16[1,2,2,32,1024]{4,3,2,1,0:T(8,128)(2,1)} %param.5) | copy-start | bytes 786436
  57.2 21.1 %all-to-all-start.1 = ((f32[32,1,2048]{2,1,0:T(1,128)}), f32[32,1,2048]{2,1,0:T(1,128)S(1)}, u32[]{:S(2)}, u32[]{:S(2)}) async-start(f32[32,1,2048]{2,1,0:T(1,128)} %reshape.343), calls=%async_computation.1 | async-start | bytes 524288 | tf_op jit(solution)/shard_map/all_to_all | solution.py:144
  84.4 1.0 copy-start.5
  92.3 21.0 %all-to-all-start.2 = ((f32[32,1,2048]{2,1,0:T(1,128)}), f32[32,1,2048]{2,1,0:T(1,128)S(1)}, u32[]{:S(2)}, u32[]{:S(2)}) async-start(f32[32,1,2048]{2,1,0:T(1,128)} %reshape.345), calls=%async_computation.2 | async-start | bytes 524288 | tf_op jit(solution)/shard_map/all_to_all | solution.py:137
  122.2 0.7 copy-start
  123.3 0.6 copy-start.10
  132.1 5.2 %copy-start.7 = (f32[1,1,32,1024]{3,2,1,0:T(8,128)S(1)}, f32[1,1,32,1024]{3,2,1,0:T(8,128)}, u32[]{:S(2)}) copy-start(f32[1,1,32,1024]{3,2,1,0:T(8,128)} %get-tuple-element.55) | copy-start | bytes 393220
  132.1 21.1 %all-to-all-start.3 = ((f32[32,1,2048]{2,1,0:T(1,128)}), f32[32,1,2048]{2,1,0:T(1,128)S(1)}, u32[]{:S(2)}, u32[]{:S(2)}) async-start(f32[32,1,2048]{2,1,0:T(1,128)} %reshape.347), calls=%async_computation.3 | async-start | bytes 524288 | tf_op jit(solution)/shard_map/all_to_all | solution.py:144
  137.3 0.9 copy-start.6
  159.3 1.0 copy-start.4
  160.2 0.9 copy-start.3
  167.6 21.1 %all-to-all-start.4 = ((f32[32,1,2048]{2,1,0:T(1,128)}), f32[32,1,2048]{2,1,0:T(1,128)S(1)}, u32[]{:S(2)}, u32[]{:S(2)}) async-start(f32[32,1,2048]{2,1,0:T(1,128)} %reshape.349), calls=%async_computation.4 | async-start | bytes 524288 | tf_op jit(solution)/shard_map/all_to_all | solution.py:137
  172.9 0.7 copy-start.11
  174.1 0.6 copy-start.13
  197.0 1.0 copy-start.1
  235.4 10.3 %copy-start.2 = (bf16[1,8,32,1024]{3,2,1,0:T(8,128)(2,1)S(1)}, bf16[1,8,32,1024]{3,2,1,0:T(8,128)(2,1)}, u32[]{:S(2)}) copy-start(bf16[1,8,32,1024]{3,2,1,0:T(8,128)(2,1)} %param.4) | copy-start | bytes 1572868
  236.1 9.6 %collective-permute-start = (f32[32,1024]{1,0:T(8,128)S(1)}, f32[32,1024]{1,0:T(8,128)S(1)}, u32[]{:S(2)}, u32[]{:S(2)}) collective-permute-start(f32[32,1024]{1,0:T(8,128)S(1)} %mul.2076), channel_id=1, source_target_pairs={{0,32},{32,64},{64,96},{96,128},{128,160},{160,192},{192,224},{224... | collective-permute-start | bytes 393224 | tf_op jit(solution)/shard_map/ppermute | solution.py:14
where the time goes:
time: 446 us; the launch traced here: 441 us
  blocking collectives  210 us (47%)
  waiting for transfers between devices  77.6 us (17%)
  local copies, waits for them, and re-layouts  44.2 us (10%)
  starting transfers between devices  41.3 us (9%)
  matrix products  38.5 us (9%)
  other arithmetic  25.3 us (6%)
    psum x1, blocking collectives, per_device(): coeffs = lax.psum(local_dots, ('seg', 'space')) / cells  95.1 us
    psum x1, blocking collectives, per_device(): norm_sq = lax.psum(jnp.sum(remainder * remainder), ('seg', 'space')) / cells  94.8 us
    all_to_all x3, waiting for transfers between devices, forward_field(): lax.all_to_all(stacked, 'space', split_axis=2, concat_axis=0, tiled=True)  42.6 us
    all_to_all x2, waiting for transfers between devices, inverse_field(): lax.all_to_all(spread, 'space', split_axis=0, concat_axis=2, tiled=True)  28.5 us
    all_to_all x3, starting transfers between devices, forward_field(): lax.all_to_all(stacked, 'space', split_axis=2, concat_axis=0, tiled=True)  27.9 us
    all_to_all x1, blocking collectives, inverse_field(): lax.all_to_all(spread, 'space', split_axis=0, concat_axis=2, tiled=True)  20.3 us
    unnamed x40, local copies, waits for them, and re-layouts  20.3 us
    dot_general x40, matrix products, product(): return jnp.einsum(form, operand, factor, precision=highest)  19.7 us
  transfers between devices with their start and end apart: 6, of which 6 were waited for; matrix products, arithmetic and copies ran while one was open for 1% of the time, Pallas kernels for 0%

commit v1 on v0

v1 whole, which is shorter than its diff:
```python
import math

import jax
import jax.numpy as jnp
import ml_dtypes
import numpy as np
from jax import lax
from jax.experimental import pallas as pl
from jax.experimental.pallas import tpu as pltpu
from jax.sharding import PartitionSpec as P

MESH = pl.DeviceIdType.MESH
GRID = 1024
SPACE = 32
SEGS = 16
KRYLOV = 8
ROWS = GRID // SPACE
HALF = math.sqrt(0.5)


def make_tables():
    tabs = {}
    small = np.arange(128)
    full = np.arange(256)
    short = np.arange(32)

    def by_owner(real, imag):
        parts = [part.reshape(part.shape[0], 32, 4) for part in (real, imag)]
        return np.stack(parts, axis=2).reshape(real.shape[0], 256)

    def owner_rows(real, imag):
        parts = [part.reshape(32, 4, -1) for part in (real, imag)]
        return np.stack(parts, axis=1).reshape(256, -1)

    def swapped(table):
        parts = table.reshape(32, 2, 4, 256)
        return np.stack([parts[:, 1], -parts[:, 0]], axis=1).reshape(256, 256)

    angle = 2 * np.pi / 256 * ((full[:, None] * small[None, :]) % 256)
    real, imag = np.cos(angle), -np.sin(angle)
    imag[:, 0] = (-1.0) ** full
    tabs["A0"] = by_owner(real, imag)
    real, imag = 2 * np.cos(angle.T), -2 * np.sin(angle.T)
    real[0], imag[0] = 1.0, (-1.0) ** full
    tabs["B0"] = owner_rows(real, imag) / GRID
    angle = 2 * np.pi / 128 * ((small[:, None] * small[None, :]) % 128)
    cos, sin = np.cos(angle), np.sin(angle)
    tabs["A1"] = np.concatenate([by_owner(cos, -sin), by_owner(sin, cos)], 0)
    real = np.concatenate([cos, sin], 1)
    imag = np.concatenate([-sin, cos], 1)
    tabs["B1"] = owner_rows(real, imag) * 2 / GRID
    tabs["D0"] = swapped(tabs["B0"])
    tabs["D1"] = swapped(tabs["B1"])
    angle = 2 * np.pi / 32 * ((short[:, None] * short[None, :]) % 32)
    cos, sin = np.cos(angle), np.sin(angle)
    table = np.zeros((2, 5, 32, 32, 2, 4))
    for low in range(4):
        table[0, low, :, :, 0, low] = cos
        table[0, low, :, :, 1, low] = sin
        table[1, low, :, :, 0, low] = -sin
        table[1, low, :, :, 1, low] = cos
    table[0, 4, :, :, 1, 0] = cos
    table[1, 4, :, :, 1, 0] = -sin
    tabs["L1"] = table.reshape(320, 256)
    table = np.zeros((32, 2, 4, 2, 4, 32))
    for low in range(4):
        table[:, 0, low, 0, low, :] = cos
        table[:, 0, low, 1, low, :] = -sin
        table[:, 1, low, 0, low, :] = sin
        table[:, 1, low, 1, low, :] = cos
    tabs["M1"] = table.reshape(256, 256) / GRID
    for name, sign in (("L2", 1.0), ("M2", -1.0)):
        table = np.zeros((2, 4, 32, 2, 4, 32))
        for slot in range(4):
            table[0, slot, :, 0, slot, :] = cos
            table[0, slot, :, 1, slot, :] = -sign * sin
            table[1, slot, :, 0, slot, :] = sign * sin
            table[1, slot, :, 1, slot, :] = cos
        tabs[name] = table.reshape(256, 256)
    return tabs


def make_constants():
    offsets, parts, at = {}, [], 0
    for name, table in make_tables().items():
        table = table.astype(np.float32)
        high = table.astype(ml_dtypes.bfloat16)
        low = (table - high.astype(np.float32)).astype(ml_dtypes.bfloat16)
        count = table.shape[0]
        offsets[name] = (at, count)
        parts += [high, low]
        at += 2 * count
    small = np.arange(128)
    short = np.arange(32)
    twist = np.zeros((96, 128))
    angle = 2 * np.pi / GRID * ((np.arange(1, 4)[:, None] * small[None, :]) % GRID)
    twist[0:3], twist[8:11] = np.cos(angle), np.sin(angle)
    angle = 2 * np.pi / GRID * ((short[:, None] * short[None, :]) % GRID)
    twist[16:48] = np.tile(np.cos(angle), (1, 4))
    twist[48:80] = np.tile(np.sin(angle), (1, 4))
    for slot in range(4):
        freq = 4 * small if slot == 0 else slot + 8 * small
        freq = np.where(freq < GRID // 2, freq, freq - GRID) * (8.0 / GRID)
        lanes = np.stack([freq.reshape(32, 4)] * 2, axis=1).reshape(256)
        twist[80 + slot], twist[88 + slot] = lanes[:128], lanes[128:]
    return offsets, np.concatenate(parts, 0), twist.astype(np.float32)


OFFSETS, TABLE, TWIST = make_constants()


def dot(left, right):
    return jnp.dot(left, right, preferred_element_type=jnp.float32)


def halves(value):
    high = value.astype(jnp.bfloat16)
    return high, (value - high.astype(jnp.float32)).astype(jnp.bfloat16)


def phi_triple(scaled):
    small = jnp.abs(scaled) < 0.5
    safe = jnp.where(small, jnp.ones_like(scaled), scaled)
    inverse = 1.0 / safe
    growth = jnp.exp(safe) - 1.0
    first_phi = growth * inverse
    second_phi = (first_phi - 1.0) * inverse
    series_one = jnp.zeros_like(scaled)
    series_two = jnp.zeros_like(scaled)
    for power in range(10, -1, -1):
        fact_one = float(math.factorial(power + 1))
        series_one = series_one * scaled + 1.0 / fact_one
        series_two = series_two * scaled + 1.0 / (fact_one * (power + 2))
    return (
        jnp.exp(scaled),
        jnp.where(small, series_one, first_phi),
        jnp.where(small, series_two, second_phi),
    )


def kernel(
    steps_ref, shift_ref, basis_hbm, grad_hbm, table_hbm, twist_hbm,
    out_ref, hess_ref,
    basis, grad, table, twist,
    s1, s2, s3, s4, s5, s6, r1, r2, r3, r4, r5, r6,
    mine, sum_a, sum_b,
    local_sem, send_sem, recv_sem, ready,
):
    seg = lax.axis_index("seg")
    me = lax.axis_index("space")
    f32 = jnp.float32

    loads = [
        pltpu.make_async_copy(source, target, local_sem.at[at])
        for at, (source, target) in enumerate(
            ((basis_hbm, basis), (twist_hbm, twist), (table_hbm, table), (grad_hbm, grad))
        )
    ]
    for load in loads:
        load.start()

    barrier = pltpu.get_barrier_semaphore()

    def greet_space(step, carry):
        peer = lax.rem(me + step, SPACE)
        pl.semaphore_signal(barrier, inc=1, device_id={"space": peer}, device_id_type=MESH)
        return carry

    def greet_seg(step, carry):
        peer = lax.rem(seg + step, SEGS)
        pl.semaphore_signal(barrier, inc=1, device_id={"seg": peer}, device_id_type=MESH)
        return carry

    lax.fori_loop(1, SPACE, greet_space, 0)
    lax.fori_loop(1, SEGS, greet_seg, 0)

    def const(name):
        at, count = OFFSETS[name]
        return table[at : at + count, :], table[at + count : at + 2 * count, :]

    def const_left(name, value):
        high, low = halves(value)
        table_high, table_low = const(name)
        both = dot(table_high, jnp.concatenate([high, low], axis=1))
        return both[:, :128] + both[:, 128:] + dot(table_low, high)

    def const_right(value, name):
        count = value.shape[0]
        high, low = halves(value)
        table_high, table_low = const(name)
        both = dot(jnp.concatenate([high, low], axis=0), table_high)
        return both[:count] + both[count:] + dot(high, table_low)

    def send(source, target, at, rows):
        def step_to(step, carry):
            peer = lax.rem(me + step, SPACE)
            pltpu.make_async_remote_copy(
                src_ref=source.at[pl.ds(pl.multiple_of(peer * rows, 8), rows)],
                dst_ref=target.at[pl.ds(pl.multiple_of(me * rows, 8), rows)],
                send_sem=send_sem.at[at],
                recv_sem=recv_sem.at[at],
                device_id={"space": peer},
                device_id_type=MESH,
            ).start()
            return carry

        lax.fori_loop(1, SPACE, step_to, 0)
        own = pl.ds(pl.multiple_of(me * rows, 8), rows)
        target[own, :] = source[own, :]

    def arrival(source, target, at, rows):
        return pltpu.make_async_remote_copy(
            src_ref=source.at[pl.ds(0, rows)],
            dst_ref=target.at[pl.ds(0, rows)],
            send_sem=send_sem.at[at],
            recv_sem=recv_sem.at[at],
            device_id={"space": me},
            device_id_type=MESH,
        )

    def row_spectrum(field):
        group = [field[:, 128 * at : 128 * at + 128] for at in range(8)]
        plus = [group[at] + group[at + 4] for at in range(4)]
        minus = [group[at] - group[at + 4] for at in range(4)]
        zero = jnp.concatenate([plus[0] + plus[2], plus[1] + plus[3]], axis=1)
        inner = HALF * (minus[1] - minus[3])
        outer = HALF * (minus[1] + minus[3])
        pairs = (
            (minus[0] + inner, -(minus[2] + outer)),
            (plus[0] - plus[2], plus[3] - plus[1]),
            (minus[0] - inner, minus[2] - outer),
        )
        rest = []
        for at, (real, imag) in enumerate(pairs):
            cos, sin = twist[at : at + 1, :], twist[8 + at : 9 + at, :]
            rest.append(
                jnp.concatenate([real * cos + imag * sin, imag * cos - real * sin], axis=1)
            )
        return const_right(zero, "A0"), const_right(jnp.concatenate(rest, axis=0), "A1")

    def row_field(zero, rest):
        turned = []
        for at in range(3):
            real, imag = rest[32 * at : 32 * at + 32, :128], rest[32 * at : 32 * at + 32, 128:]
            cos, sin = twist[at : at + 1, :], twist[8 + at : 9 + at, :]
            turned.append((real * cos - imag * sin, real * sin + imag * cos))
        (re1, im1), (re2, im2), (re3, im3) = turned
        even, odd = zero[:, :128], zero[:, 128:]
        sums = (even + re2, odd - im2, even - re2, odd + im2)
        differences = (
            re1 + re3,
            HALF * ((re1 - im1) - (re3 + im3)),
            im3 - im1,
            HALF * ((re3 - im3) - (re1 + im1)),
        )
        pieces = [sums[at] + differences[at] for at in range(4)]
        pieces += [sums[at] - differences[at] for at in range(4)]
        return jnp.concatenate(pieces, axis=1)

    def rows_forward(field, target):
        zero, rest = row_spectrum(field)
        target[...] = jnp.concatenate([zero, rest], axis=0).T
        return zero, rest

    def rows_inverse(received):
        turned = received.T
        return row_field(const_right(turned[:32], "B0"), const_right(turned[32:], "B1"))

    def stacked(value):
        return jnp.concatenate([value] * 5, axis=0)

    lane = lax.broadcasted_iota(jnp.int32, (160, 128), 1)
    row = lax.broadcasted_iota(jnp.int32, (160, 128), 0)
    anchor = jnp.where((lane[:32] < 32) & (me == 0), 1.0, 0.0).astype(f32)

    def columns_forward(received):
        value = const_left("L1", received)
        real, imag = value[:160], value[160:]
        real = jnp.concatenate([real[:32] + anchor * imag[128:], real[32:]], axis=0)
        imag = jnp.concatenate([imag[:32] - anchor * value[128:160], imag[32:]], axis=0)
        cos, sin = stacked(twist[16:48, :]), stacked(twist[48:80, :])
        turned = jnp.concatenate([real * cos + imag * sin, imag * cos - real * sin], axis=1)
        value = const_right(turned, "L2")
        return value[:, :128], value[:, 128:]

    def columns_inverse(real, imag):
        value = const_right(jnp.concatenate([real, imag], axis=1), "M2")
        real, imag = value[:, :128], value[:, 128:]
        cos, sin = stacked(twist[16:48, :]), stacked(twist[48:80, :])
        real, imag = real * cos - imag * sin, real * sin + imag * cos
        value = jnp.concatenate(
            [real[:32] - anchor * imag[128:], real[32:128], imag[:32] + anchor * real[128:], imag[32:128]],
            axis=0,
        )
        return const_left("M1", value)

    loads[0].wait()
    loads[1].wait()
    loads[2].wait()
    start = basis[KRYLOV - 1].astype(f32)
    zero, rest = rows_forward(start, s1)
    pl.semaphore_wait(barrier, SPACE + SEGS - 2)
    pl.semaphore_signal(
        ready, inc=1, device_id={"seg": lax.rem(seg + SEGS - 1, SEGS)}, device_id_type=MESH
    )
    send(s1, r1, 0, 8)

    waves = [
        jnp.concatenate([twist[80 + at : 81 + at, :], twist[88 + at : 89 + at, :]], axis=1)
        for at in range(4)
    ]
    lifted = jnp.concatenate([rest[32 * at : 32 * at + 32] * waves[at + 1] for at in range(3)], axis=0)
    grad_y = row_field(const_right(zero * waves[0], "D0"), const_right(lifted, "D1"))

    slot = lane // 32
    low = row // 32
    freq_x = row % 32 + 32 * (lane % 32)
    base = 4 * me + low
    freq_y = jnp.where(low == 4, GRID // 2, jnp.where(slot == 0, 4 * base, slot + 8 * base))
    signed_x = jnp.where(freq_x < GRID // 2, freq_x, freq_x - GRID)
    signed_y = jnp.where(freq_y < GRID // 2, freq_y, freq_y - GRID)
    wave_x = signed_x.astype(f32) * (8.0 / GRID)
    wave_y = signed_y.astype(f32) * (8.0 / GRID)
    deriv_x = jnp.where(signed_x == -(GRID // 2), 0.0, wave_x)
    deriv_y = jnp.where(signed_y == -(GRID // 2), 0.0, wave_y)
    squared = wave_x * wave_x + wave_y * wave_y
    step_size = 0.01 * steps_ref[0].astype(f32)
    decay, phi_one, phi_two = phi_triple((squared - squared * squared) * step_size)
    phi_one = step_size * phi_one
    phi_two = step_size * phi_two

    done = arrival(s1, r1, 0, 248)
    done.wait_recv()
    state_re, state_im = columns_forward(r1[...])

    s2[...] = columns_inverse(-deriv_x * state_im, deriv_x * state_re)
    send(s2, r2, 1, 8)
    loads[3].wait()
    part_y = grad[1].astype(f32) * grad_y
    part_x = -grad[0].astype(f32)
    arrival(s2, r2, 1, 248).wait_recv()
    term = part_x * rows_inverse(r2[...]) - part_y

    rows_forward(term, s3)
    send(s3, r3, 2, 8)
    flat = basis[...].reshape(KRYLOV * ROWS, GRID)
    gram = lax.dot_general(flat, flat, (((1,), (1,)), ((), ())), preferred_element_type=f32)
    gram_row = lax.broadcasted_iota(jnp.int32, (256, 256), 0)
    gram_lane = lax.broadcasted_iota(jnp.int32, (256, 256), 1)
    gram = jnp.where(gram_row % 32 == gram_lane % 32, gram, 0.0)
    gram = jnp.concatenate(
        [jnp.sum(gram[32 * at : 32 * at + 32], axis=0, keepdims=True) for at in range(8)], axis=0
    )
    spot_row = lax.broadcasted_iota(jnp.int32, (8, 128), 0)
    spot_lane = lax.broadcasted_iota(jnp.int32, (8, 128), 1)
    gram_sums = jnp.zeros((8, 128), f32)
    for at in range(8):
        part = jnp.sum(jnp.where(gram_lane[:8] // 32 == at, gram, 0.0), axis=1, keepdims=True)
        gram_sums = gram_sums + jnp.where(spot_lane == 16 + 8 * spot_row + at, part, 0.0)
    gram_sums = jnp.sum(gram_sums, axis=0, keepdims=True)
    arrival(s3, r3, 2, 248).wait_recv()
    term_re, term_im = columns_forward(r3[...])
    middle_re = decay * state_re + phi_one * term_re
    middle_im = decay * state_im + phi_one * term_im

    toward_x = columns_inverse(-deriv_x * middle_im, deriv_x * middle_re)
    toward_y = columns_inverse(-deriv_y * middle_im, deriv_y * middle_re)
    for peer in range(SPACE):
        s4[16 * peer : 16 * peer + 8, :] = toward_x[8 * peer : 8 * peer + 8]
        s4[16 * peer + 8 : 16 * peer + 16, :] = toward_y[8 * peer : 8 * peer + 8]
    send(s4, r4, 3, 16)
    offset = (freq_x * shift_ref[0] + freq_y * shift_ref[1]) & (GRID - 1)
    angle = (2.0 * math.pi / GRID) * offset.astype(f32)
    is_last = seg == SEGS - 1
    cosine = jnp.where(is_last, jnp.cos(angle), 1.0)
    sine = jnp.where(is_last, jnp.sin(angle), 0.0)
    arrival(s4, r4, 3, 496).wait_recv()
    got_x = jnp.concatenate([r4[16 * peer : 16 * peer + 8, :] for peer in range(SPACE)], axis=0)
    got_y = jnp.concatenate([r4[16 * peer + 8 : 16 * peer + 16, :] for peer in range(SPACE)], axis=0)
    term = -(grad[2].astype(f32) * rows_inverse(got_x) + grad[3].astype(f32) * rows_inverse(got_y))

    rows_forward(term, s5)
    send(s5, r5, 4, 8)
    kept_re = middle_re - phi_two * term_re
    kept_im = middle_im - phi_two * term_im
    arrival(s5, r5, 4, 248).wait_recv()
    term_re, term_im = columns_forward(r5[...])
    state_re = kept_re + phi_two * term_re
    state_im = kept_im + phi_two * term_im

    s6[...] = columns_inverse(cosine * state_re + sine * state_im, cosine * state_im - sine * state_re)
    pl.semaphore_wait(ready, 1)
    next_seg = lax.rem(seg + 1, SEGS)

    def onward(step, carry):
        peer = lax.rem(me + step, SPACE)
        pltpu.make_async_remote_copy(
            src_ref=s6.at[pl.ds(pl.multiple_of(peer * 8, 8), 8)],
            dst_ref=r6.at[pl.ds(pl.multiple_of(me * 8, 8), 8)],
            send_sem=send_sem.at[5],
            recv_sem=recv_sem.at[5],
            device_id={"seg": next_seg, "space": peer},
            device_id_type=MESH,
        ).start()
        return carry

    lax.fori_loop(0, SPACE, onward, 0)
    arrival(s6, r6, 5, 256).wait_recv()
    wrapped = rows_inverse(r6[...]) - start

    def folded(value):
        total = value[:, :128]
        for at in range(1, 8):
            total = total + value[:, 128 * at : 128 * at + 128]
        return jnp.sum(total, axis=0, keepdims=True)

    lines = [folded(wrapped * basis[at].astype(f32)) for at in range(KRYLOV)]
    lines.append(folded(wrapped * wrapped))
    lines.append(jnp.zeros((7, 128), f32))
    sums = jnp.sum(jnp.concatenate(lines, axis=0), axis=1, keepdims=True)
    spot_row = lax.broadcasted_iota(jnp.int32, (16, 128), 0)
    spot_lane = lax.broadcasted_iota(jnp.int32, (16, 128), 1)
    line = jnp.sum(jnp.where(spot_row == spot_lane, sums, 0.0), axis=0, keepdims=True) + gram_sums

    def spread(target, axis, count, own, at):
        target[own] = mine[at]

        def step_to(step, carry):
            peer = lax.rem(own + step, count)
            pltpu.make_async_remote_copy(
                src_ref=mine.at[at],
                dst_ref=target.at[own],
                send_sem=send_sem.at[6 + at],
                recv_sem=recv_sem.at[6 + at],
                device_id={axis: peer},
                device_id_type=MESH,
            ).start()
            return carry

        lax.fori_loop(1, count, step_to, 0)
        done = pltpu.make_async_remote_copy(
            src_ref=target.at[pl.ds(0, count - 1)],
            dst_ref=target.at[pl.ds(0, count - 1)],
            send_sem=send_sem.at[6 + at],
            recv_sem=recv_sem.at[6 + at],
            device_id={axis: own},
            device_id_type=MESH,
        )
        done.wait_recv()
        return done, jnp.sum(target[...], axis=0)

    mine[0] = line
    sent_a, line = spread(sum_a, "space", SPACE, me, 0)
    mine[1] = line
    sent_b, line = spread(sum_b, "seg", SEGS, seg, 1)
    line = line * (1.0 / (SEGS * GRID * GRID))

    lanes = lax.broadcasted_iota(jnp.int32, (1, 128), 1)

    def lane_of(at):
        return jnp.sum(jnp.where(lanes == at, line, 0.0), axis=1, keepdims=True)

    coeffs = [lane_of(at) for at in range(KRYLOV)]
    norm_sq = lane_of(KRYLOV)
    left = jnp.zeros((1, 128), f32)
    right = jnp.zeros((1, 128), f32)
    for at in range(KRYLOV):
        left = left + jnp.where((lanes >= 16 + 8 * at) & (lanes < 24 + 8 * at), coeffs[at], 0.0)
        right = right + jnp.where((lanes >= 16) & (lanes % 8 == at) & (lanes < 80), coeffs[at], 0.0)
        norm_sq = norm_sq - 2.0 * coeffs[at] * coeffs[at]
    norm_sq = norm_sq + jnp.sum(left * right * line, axis=1, keepdims=True)
    norm = jnp.sqrt(norm_sq)
    hess_ref[...] = jnp.where(lanes == KRYLOV, norm, line)
    inverse = 1.0 / norm
    remainder = wrapped
    for at in range(KRYLOV):
        remainder = remainder - coeffs[at] * basis[at].astype(f32)
    out_ref[0] = remainder * inverse

    for source, at, rows in ((s1, 0, 248), (s2, 1, 248), (s3, 2, 248), (s4, 3, 496), (s5, 4, 248), (s6, 5, 256)):
        arrival(source, source, at, rows).wait_send()
    sent_a.wait_send()
    sent_b.wait_send()


def per_device(basis, base_grad, step_counts, shift):
    any_space = pl.BlockSpec(memory_space=pl.ANY)
    scalars = pl.BlockSpec(memory_space=pltpu.SMEM)
    f32, bf16 = jnp.float32, jnp.bfloat16
    tile = pltpu.VMEM((256, 128), f32)
    wide = pltpu.VMEM((512, 128), f32)
    new_vector, line = pl.pallas_call(
        kernel,
        out_shape=(
            jax.ShapeDtypeStruct((1, ROWS, GRID), f32),
            jax.ShapeDtypeStruct((1, 128), f32),
        ),
        in_specs=[scalars, scalars] + [any_space] * 4,
        out_specs=(pl.BlockSpec(memory_space=pltpu.VMEM),) * 2,
        scratch_shapes=[
            pltpu.VMEM((KRYLOV, ROWS, GRID), bf16),
            pltpu.VMEM((4, ROWS, GRID), bf16),
            pltpu.VMEM(TABLE.shape, bf16),
            pltpu.VMEM(TWIST.shape, f32),
            tile, tile, tile, wide, tile, tile,
            tile, tile, tile, wide, tile, tile,
            pltpu.VMEM((2, 1, 128), f32),
            pltpu.VMEM((SPACE, 1, 128), f32),
            pltpu.VMEM((SEGS, 1, 128), f32),
            pltpu.SemaphoreType.DMA((4,)),
            pltpu.SemaphoreType.DMA((8,)),
            pltpu.SemaphoreType.DMA((8,)),
            pltpu.SemaphoreType.REGULAR,
        ],
        compiler_params=pltpu.CompilerParams(
            collective_id=0, has_side_effects=True, vmem_limit_bytes=40 * 1024 * 1024
        ),
    )(
        step_counts,
        shift,
        basis[0],
        base_grad.reshape(4, ROWS, GRID),
        jnp.asarray(TABLE),
        jnp.asarray(TWIST),
    )
    return new_vector, line[0, : KRYLOV + 1]


def solution(mesh):
    in_specs = (P("seg", None, "space", None), P("seg", None, None, "space", None), P("seg"), P())
    out_specs = (P("seg", "space", None), P())
    return jax.shard_map(
        per_device, mesh=mesh, in_specs=in_specs, out_specs=out_specs, check_vma=False
    )
```

time: 446 us -> 94.1 us (0.21); the launches traced: 441 us -> 93.8 us
  blocking collectives: 210 us -> 0 us
  Pallas kernels: 0 us -> 86.1 us
  waiting for transfers between devices: 77.6 us -> 0 us
  starting transfers between devices: 41.3 us -> 0 us
  matrix products: 38.5 us -> 0 us
  local copies, waits for them, and re-layouts: 44.2 us -> 6.37 us
  other arithmetic: 25.3 us -> 0 us
    psum x2 -> x0, blocking collectives: 190 us -> none  [the longest x1 95.1 us: per_device(): coeffs = lax.psum(local_dots, ('seg', 'space')) / cells]
    pallas_call x0 -> x1, Pallas kernels: none -> 86.1 us  [per_device(): pl.pallas_call(kernel, out_shape=(jax.ShapeDtypeStruct((1, ROWS, GRID), f...]
    all_to_all x5 -> x0, waiting for transfers between devices: 71.1 us -> none  [the longest x3 42.6 us: forward_field(): lax.all_to_all(stacked, 'space', split_axis=2, concat_axis=0, tiled=True)]
    all_to_all x5 -> x0, starting transfers between devices: 38.2 us -> none  [the longest x3 27.9 us: forward_field(): lax.all_to_all(stacked, 'space', split_axis=2, concat_axis=0, tiled=True)]
    dot_general x54 -> x0, matrix products: 30.1 us -> none  [the longest x40 19.7 us: product(): return jnp.einsum(form, operand, factor, precision=highest)]
    all_to_all x1 -> x0, blocking collectives: 20.3 us -> none  [inverse_field(): lax.all_to_all(spread, 'space', split_axis=0, concat_axis=2, tiled=True)]
    unnamed x40 -> x11, local copies, waits for them, and re-layouts: 20.3 us -> 5.85 us
    unnamed x12 -> x0, matrix products: 8.39 us -> none
  transfers between devices with their start and end apart: 6 -> 0, of which waited for: 6 -> 0; matrix products, arithmetic and copies ran while one was open for 1% -> 0% of each run, Pallas kernels for 0% -> 0%
where the time goes in v1:
time: 94.1 us; the launch traced here: 93.8 us
  Pallas kernels  86.1 us (91%)
  local copies, waits for them, and re-layouts  6.37 us (7%)
  between operations  1.3 us (1%)
    pallas_call x1, Pallas kernels, per_device(): pl.pallas_call(kernel, out_shape=(jax.ShapeDtypeStruct((1, ROWS, GRID), f...  86.1 us
    unnamed x11, local copies, waits for them, and re-layouts  5.85 us

profile of v1, /device:TPU:1, one launch (start us, length us, event | category | flops | bytes accessed | tf_op | source)
XLA Modules:
  0.0 93.8 jit_solution(11112395486978950382)
XLA Ops:
  1.3 0.0 copy-start
  1.3 1.7 %copy-done = bf16[5248,256]{1,0:T(8,128)(2,1)S(1)} copy-done((bf16[5248,256]{1,0:T(8,128)(2,1)S(1)}, bf16[5248,256]{1,0:T(8,128)(2,1)}, u32[]{:S(2)}) %copy-start) | copy-done | bytes 2687000
  3.0 0.0 copy-start.1
  3.0 1.0 %copy-done.1 = bf16[1,8,32,1024]{3,2,1,0:T(8,128)(2,1)S(1)} copy-done((bf16[1,8,32,1024]{3,2,1,0:T(8,128)(2,1)S(1)}, bf16[1,8,32,1024]{3,2,1,0:T(8,128)(2,1)}, u32[]{:S(2)}) %copy-start.1) | copy-done | bytes 524312
  4.1 0.0 copy-start.2
  4.1 0.9 %copy-done.2 = bf16[1,2,2,32,1024]{4,3,2,1,0:T(8,128)(2,1)S(1)} copy-done((bf16[1,2,2,32,1024]{4,3,2,1,0:T(8,128)(2,1)S(1)}, bf16[1,2,2,32,1024]{4,3,2,1,0:T(8,128)(2,1)}, u32[]{:S(2)}) %copy-start.2) | copy-done | bytes 262168
  5.0 0.0 copy-start.3
  5.0 0.8 copy-done.3
  5.8 0.0 copy-start.4
  5.8 0.7 copy-done.4
  6.5 86.1 %shard_map.77 = (f32[1,32,1024]{2,1,0:T(8,128)S(1)}, f32[1,128]{1,0:T(1,128)S(1)}) custom-call(s32[1]{0:T(128)S(6)} %copy.9.steps_ref, s32[2]{0:T(128)S(1)} %copy-done.4, bf16[8,32,1024]{2,1,0:T(8,128)(2,1)S(1)} %bitcast.4, bf16[4,32,1024]{2,1,0:T(8,128)(2,1)S(1)} %bitcast.5, bf16[5248,256]{1,0:T(8,128)(2,1)S(1)} %copy-done, f32[96,128]{1,0:T(8,128)S(1)} %copy-done.3), custom_call_target="tpu_custom_call" | custom-call | tf_op jit(solution)/shard_map/pallas_call | solution.py:492
  92.6 0.5 slice_bitcast_fusion
  93.2 0.7 copy.10
Async XLA Ops:
  1.3 1.8 %copy-start = (bf16[5248,256]{1,0:T(8,128)(2,1)S(1)}, bf16[5248,256]{1,0:T(8,128)(2,1)}, u32[]{:S(2)}) copy-start(bf16[5248,256]{1,0:T(8,128)(2,1)} %constant.4.clone.table_hbm) | copy-start | bytes 8060932
  3.0 1.0 %copy-start.1 = (bf16[1,8,32,1024]{3,2,1,0:T(8,128)(2,1)S(1)}, bf16[1,8,32,1024]{3,2,1,0:T(8,128)(2,1)}, u32[]{:S(2)}) copy-start(bf16[1,8,32,1024]{3,2,1,0:T(8,128)(2,1)} %param.6) | copy-start | bytes 1572868
  4.1 0.9 %copy-start.2 = (bf16[1,2,2,32,1024]{4,3,2,1,0:T(8,128)(2,1)S(1)}, bf16[1,2,2,32,1024]{4,3,2,1,0:T(8,128)(2,1)}, u32[]{:S(2)}) copy-start(bf16[1,2,2,32,1024]{4,3,2,1,0:T(8,128)(2,1)} %param.7) | copy-start | bytes 786436
  5.0 0.8 copy-start.3
  5.8 0.7 copy-start.4

commit v2 on v1

--- a/solution.py
+++ b/solution.py
@@ -14,6 +14,8 @@
 SPACE = 32
 SEGS = 16
 KRYLOV = 8
+PLANE = 32
+COLUMN = 16
 ROWS = GRID // SPACE
 HALF = math.sqrt(0.5)
 
@@ -141,13 +143,17 @@
 def kernel(
     steps_ref, shift_ref, basis_hbm, grad_hbm, table_hbm, twist_hbm,
     out_ref, hess_ref,
-    basis, grad, table, twist,
+    basis, grad, table, twist, counts,
     s1, s2, s3, s4, s5, s6, r1, r2, r3, r4, r5, r6,
     mine, sum_a, sum_b,
     local_sem, send_sem, recv_sem, ready,
 ):
     seg = lax.axis_index("seg")
     me = lax.axis_index("space")
+    other = seg + 2 - 4 * (lax.rem(seg, 4) // 2)
+    half, place = me // 16, lax.rem(me, 16)
+    column_y, core = place // 2, lax.rem(place, 2)
+    chip_x, chip_z = seg // 4, lax.rem(seg, 4) + 4 * half
     f32 = jnp.float32
 
     loads = [
@@ -159,20 +165,44 @@
     for load in loads:
         load.start()
 
+    before = lax.rem(seg + SEGS - 1, SEGS)
+    before = before + 2 - 4 * (lax.rem(before, 4) // 2)
+    after = lax.rem(other + 1, SEGS)
+
     barrier = pltpu.get_barrier_semaphore()
 
+    def far_first(step, size):
+        away = (step + 1) // 2
+        return lax.rem(size + size // 2 + away * (1 - 2 * lax.rem(step, 2)), size)
+
+    def peer_in_space(step):
+        inner = lax.rem(step, 4)
+        chip_y = lax.rem(column_y + far_first(step // 4, 8), 8)
+        peer_core = lax.rem(core + 1 + lax.rem(inner, 2), 2)
+        return 16 * (inner // 2) + 2 * chip_y + peer_core
+
+    def peer_in_plane(step):
+        peer_z = lax.rem(chip_z + far_first(step // 4, 8), 8)
+        peer_x = lax.rem(chip_x + far_first(lax.rem(step, 4), 4), 4)
+        return {"seg": 4 * peer_x + lax.rem(peer_z, 4), "space": 16 * (peer_z // 4) + place}
+
+    def peer_in_column(step):
+        chip_y = lax.rem(column_y + far_first(step // 2, 8), 8)
+        peer_core = lax.rem(core + 1 + lax.rem(step, 2), 2)
+        return {"space": 16 * half + 2 * chip_y + peer_core}
+
     def greet_space(step, carry):
-        peer = lax.rem(me + step, SPACE)
-        pl.semaphore_signal(barrier, inc=1, device_id={"space": peer}, device_id_type=MESH)
+        pl.semaphore_signal(
+            barrier, inc=1, device_id={"seg": other, "space": peer_in_space(step)}, device_id_type=MESH
+        )
         return carry
 
-    def greet_seg(step, carry):
-        peer = lax.rem(seg + step, SEGS)
-        pl.semaphore_signal(barrier, inc=1, device_id={"seg": peer}, device_id_type=MESH)
+    def greet_plane(step, carry):
+        pl.semaphore_signal(barrier, inc=1, device_id=peer_in_plane(step), device_id_type=MESH)
         return carry
 
-    lax.fori_loop(1, SPACE, greet_space, 0)
-    lax.fori_loop(1, SEGS, greet_seg, 0)
+    lax.fori_loop(0, SPACE, greet_space, 0)
+    lax.fori_loop(0, PLANE - 1, greet_plane, 0)
 
     def const(name):
         at, count = OFFSETS[name]
@@ -191,22 +221,20 @@
         both = dot(jnp.concatenate([high, low], axis=0), table_high)
         return both[:count] + both[count:] + dot(high, table_low)
 
-    def send(source, target, at, rows):
+    def send(source, target, at, rows, to_seg):
         def step_to(step, carry):
-            peer = lax.rem(me + step, SPACE)
+            peer = peer_in_space(step)
             pltpu.make_async_remote_copy(
                 src_ref=source.at[pl.ds(pl.multiple_of(peer * rows, 8), rows)],
                 dst_ref=target.at[pl.ds(pl.multiple_of(me * rows, 8), rows)],
                 send_sem=send_sem.at[at],
                 recv_sem=recv_sem.at[at],
-                device_id={"space": peer},
+                device_id={"seg": to_seg, "space": peer},
                 device_id_type=MESH,
             ).start()
             return carry
 
-        lax.fori_loop(1, SPACE, step_to, 0)
-        own = pl.ds(pl.multiple_of(me * rows, 8), rows)
-        target[own, :] = source[own, :]
+        lax.fori_loop(0, SPACE, step_to, 0)
 
     def arrival(source, target, at, rows):
         return pltpu.make_async_remote_copy(
@@ -299,11 +327,18 @@
     loads[2].wait()
     start = basis[KRYLOV - 1].astype(f32)
     zero, rest = rows_forward(start, s1)
-    pl.semaphore_wait(barrier, SPACE + SEGS - 2)
-    pl.semaphore_signal(
-        ready, inc=1, device_id={"seg": lax.rem(seg + SEGS - 1, SEGS)}, device_id_type=MESH
+    pl.semaphore_wait(barrier, SPACE + PLANE - 1)
+    counts[0] = jnp.full((1, 128), steps_ref[0], jnp.int32)
+    count_copy = pltpu.make_async_remote_copy(
+        src_ref=counts.at[0],
+        dst_ref=counts.at[1],
+        send_sem=send_sem.at[8],
+        recv_sem=recv_sem.at[8],
+        device_id={"seg": other},
+        device_id_type=MESH,
     )
-    send(s1, r1, 0, 8)
+    count_copy.start()
+    send(s1, r1, 0, 8, other)
 
     waves = [
         jnp.concatenate([twist[80 + at : 81 + at, :], twist[88 + at : 89 + at, :]], axis=1)
@@ -324,25 +359,27 @@
     deriv_x = jnp.where(signed_x == -(GRID // 2), 0.0, wave_x)
     deriv_y = jnp.where(signed_y == -(GRID // 2), 0.0, wave_y)
     squared = wave_x * wave_x + wave_y * wave_y
-    step_size = 0.01 * steps_ref[0].astype(f32)
+    count_copy.wait_recv()
+    step_size = 0.01 * counts[1].astype(f32)
     decay, phi_one, phi_two = phi_triple((squared - squared * squared) * step_size)
     phi_one = step_size * phi_one
     phi_two = step_size * phi_two
 
-    done = arrival(s1, r1, 0, 248)
+    done = arrival(s1, r1, 0, 256)
     done.wait_recv()
     state_re, state_im = columns_forward(r1[...])
 
     s2[...] = columns_inverse(-deriv_x * state_im, deriv_x * state_re)
-    send(s2, r2, 1, 8)
+    send(s2, r2, 1, 8, other)
     loads[3].wait()
     part_y = grad[1].astype(f32) * grad_y
     part_x = -grad[0].astype(f32)
-    arrival(s2, r2, 1, 248).wait_recv()
+    arrival(s2, r2, 1, 256).wait_recv()
+    pl.semaphore_signal(ready, inc=1, device_id={"seg": before}, device_id_type=MESH)
     term = part_x * rows_inverse(r2[...]) - part_y
 
     rows_forward(term, s3)
-    send(s3, r3, 2, 8)
+    send(s3, r3, 2, 8, other)
     flat = basis[...].reshape(KRYLOV * ROWS, GRID)
     gram = lax.dot_general(flat, flat, (((1,), (1,)), ((), ())), preferred_element_type=f32)
     gram_row = lax.broadcasted_iota(jnp.int32, (256, 256), 0)
@@ -358,7 +395,7 @@
         part = jnp.sum(jnp.where(gram_lane[:8] // 32 == at, gram, 0.0), axis=1, keepdims=True)
         gram_sums = gram_sums + jnp.where(spot_lane == 16 + 8 * spot_row + at, part, 0.0)
     gram_sums = jnp.sum(gram_sums, axis=0, keepdims=True)
-    arrival(s3, r3, 2, 248).wait_recv()
+    arrival(s3, r3, 2, 256).wait_recv()
     term_re, term_im = columns_forward(r3[...])
     middle_re = decay * state_re + phi_one * term_re
     middle_im = decay * state_im + phi_one * term_im
@@ -368,43 +405,29 @@
     for peer in range(SPACE):
         s4[16 * peer : 16 * peer + 8, :] = toward_x[8 * peer : 8 * peer + 8]
         s4[16 * peer + 8 : 16 * peer + 16, :] = toward_y[8 * peer : 8 * peer + 8]
-    send(s4, r4, 3, 16)
+    send(s4, r4, 3, 16, other)
     offset = (freq_x * shift_ref[0] + freq_y * shift_ref[1]) & (GRID - 1)
     angle = (2.0 * math.pi / GRID) * offset.astype(f32)
-    is_last = seg == SEGS - 1
+    is_last = other == SEGS - 1
     cosine = jnp.where(is_last, jnp.cos(angle), 1.0)
     sine = jnp.where(is_last, jnp.sin(angle), 0.0)
-    arrival(s4, r4, 3, 496).wait_recv()
+    arrival(s4, r4, 3, 512).wait_recv()
     got_x = jnp.concatenate([r4[16 * peer : 16 * peer + 8, :] for peer in range(SPACE)], axis=0)
     got_y = jnp.concatenate([r4[16 * peer + 8 : 16 * peer + 16, :] for peer in range(SPACE)], axis=0)
     term = -(grad[2].astype(f32) * rows_inverse(got_x) + grad[3].astype(f32) * rows_inverse(got_y))
 
     rows_forward(term, s5)
-    send(s5, r5, 4, 8)
+    send(s5, r5, 4, 8, other)
     kept_re = middle_re - phi_two * term_re
     kept_im = middle_im - phi_two * term_im
-    arrival(s5, r5, 4, 248).wait_recv()
+    arrival(s5, r5, 4, 256).wait_recv()
     term_re, term_im = columns_forward(r5[...])
     state_re = kept_re + phi_two * term_re
     state_im = kept_im + phi_two * term_im
 
     s6[...] = columns_inverse(cosine * state_re + sine * state_im, cosine * state_im - sine * state_re)
     pl.semaphore_wait(ready, 1)
-    next_seg = lax.rem(seg + 1, SEGS)
-
-    def onward(step, carry):
-        peer = lax.rem(me + step, SPACE)
-        pltpu.make_async_remote_copy(
-            src_ref=s6.at[pl.ds(pl.multiple_of(peer * 8, 8), 8)],
-            dst_ref=r6.at[pl.ds(pl.multiple_of(me * 8, 8), 8)],
-            send_sem=send_sem.at[5],
-            recv_sem=recv_sem.at[5],
-            device_id={"seg": next_seg, "space": peer},
-            device_id_type=MESH,
-        ).start()
-        return carry
-
-    lax.fori_loop(0, SPACE, onward, 0)
+    send(s6, r6, 5, 8, after)
     arrival(s6, r6, 5, 256).wait_recv()
     wrapped = rows_inverse(r6[...]) - start
 
@@ -422,37 +445,36 @@
     spot_lane = lax.broadcasted_iota(jnp.int32, (16, 128), 1)
     line = jnp.sum(jnp.where(spot_row == spot_lane, sums, 0.0), axis=0, keepdims=True) + gram_sums
 
-    def spread(target, axis, count, own, at):
+    def spread(target, peer_of, own, count, at):
         target[own] = mine[at]
 
         def step_to(step, carry):
-            peer = lax.rem(own + step, count)
             pltpu.make_async_remote_copy(
                 src_ref=mine.at[at],
                 dst_ref=target.at[own],
                 send_sem=send_sem.at[6 + at],
                 recv_sem=recv_sem.at[6 + at],
-                device_id={axis: peer},
+                device_id=peer_of(step),
                 device_id_type=MESH,
             ).start()
             return carry
 
-        lax.fori_loop(1, count, step_to, 0)
+        lax.fori_loop(0, count - 1, step_to, 0)
         done = pltpu.make_async_remote_copy(
             src_ref=target.at[pl.ds(0, count - 1)],
             dst_ref=target.at[pl.ds(0, count - 1)],
             send_sem=send_sem.at[6 + at],
             recv_sem=recv_sem.at[6 + at],
-            device_id={axis: own},
+            device_id={"seg": other},
             device_id_type=MESH,
         )
         done.wait_recv()
         return done, jnp.sum(target[...], axis=0)
 
     mine[0] = line
-    sent_a, line = spread(sum_a, "space", SPACE, me, 0)
+    sent_a, line = spread(sum_a, peer_in_column, place, COLUMN, 0)
     mine[1] = line
-    sent_b, line = spread(sum_b, "seg", SEGS, seg, 1)
+    sent_b, line = spread(sum_b, peer_in_plane, 8 * chip_x + chip_z, PLANE, 1)
     line = line * (1.0 / (SEGS * GRID * GRID))
 
     lanes = lax.broadcasted_iota(jnp.int32, (1, 128), 1)
@@ -477,10 +499,11 @@
         remainder = remainder - coeffs[at] * basis[at].astype(f32)
     out_ref[0] = remainder * inverse
 
-    for source, at, rows in ((s1, 0, 248), (s2, 1, 248), (s3, 2, 248), (s4, 3, 496), (s5, 4, 248), (s6, 5, 256)):
+    for source, at, rows in ((s1, 0, 256), (s2, 1, 256), (s3, 2, 256), (s4, 3, 512), (s5, 4, 256), (s6, 5, 256)):
         arrival(source, source, at, rows).wait_send()
     sent_a.wait_send()
     sent_b.wait_send()
+    count_copy.wait_send()
 
 
 def per_device(basis, base_grad, step_counts, shift):
@@ -502,18 +525,19 @@
             pltpu.VMEM((4, ROWS, GRID), bf16),
             pltpu.VMEM(TABLE.shape, bf16),
             pltpu.VMEM(TWIST.shape, f32),
+            pltpu.VMEM((2, 1, 128), jnp.int32),
             tile, tile, tile, wide, tile, tile,
             tile, tile, tile, wide, tile, tile,
             pltpu.VMEM((2, 1, 128), f32),
-            pltpu.VMEM((SPACE, 1, 128), f32),
-            pltpu.VMEM((SEGS, 1, 128), f32),
+            pltpu.VMEM((COLUMN, 1, 128), f32),
+            pltpu.VMEM((PLANE, 1, 128), f32),
             pltpu.SemaphoreType.DMA((4,)),
-            pltpu.SemaphoreType.DMA((8,)),
-            pltpu.SemaphoreType.DMA((8,)),
+            pltpu.SemaphoreType.DMA((9,)),
+            pltpu.SemaphoreType.DMA((9,)),
             pltpu.SemaphoreType.REGULAR,
         ],
         compiler_params=pltpu.CompilerParams(
-            collective_id=0, has_side_effects=True, vmem_limit_bytes=40 * 1024 * 1024
+            collective_id=0, has_side_effects=True, vmem_limit_bytes=62 * 1024 * 1024
         ),
     )(
         step_counts,

time: 94.1 us -> 84.1 us (0.89)
  Pallas kernels: 86.1 us -> 79.9 us
  local copies, waits for them, and re-layouts: 6.37 us -> 2.74 us
    pallas_call x1, Pallas kernels: 86.1 us -> 79.9 us  [per_device(): pl.pallas_call(kernel, out_shape=(jax.ShapeDtypeStruct((1, ROWS, GRID), f...]
    unnamed x11 -> x1, local copies, waits for them, and re-layouts: 5.85 us -> 1.57 us
where the time goes in v2:
time: 84.1 us; the launch traced here: 83.9 us
  Pallas kernels  79.9 us (95%)
  local copies, waits for them, and re-layouts  2.74 us (3%)
  between operations  1.28 us (2%)
    pallas_call x1, Pallas kernels, per_device(): pl.pallas_call(kernel, out_shape=(jax.ShapeDtypeStruct((1, ROWS, GRID), f...  79.9 us

profile of v2, /device:TPU:1, one launch (start us, length us, event | category | flops | bytes accessed | tf_op | source)
XLA Modules:
  0.0 83.9 jit_solution(5068350457182237545)
XLA Ops:
  1.3 79.9 %shard_map.77 = (f32[1,32,1024]{2,1,0:T(8,128)}, f32[1,128]{1,0:T(1,128)}) custom-call(s32[1]{0:T(128)S(6)} %copy.9.steps_ref, s32[2]{0:T(128)} %shift_ref.1, bf16[8,32,1024]{2,1,0:T(8,128)(2,1)} %bitcast.4, bf16[4,32,1024]{2,1,0:T(8,128)(2,1)} %bitcast.5, bf16[5248,256]{1,0:T(8,128)(2,1)} %constant.4.clone.table_hbm, f32[96,128]{1,0:T(8,128)} %constant.5.clone.twist_hbm), custom_call_target="tpu_custom_call" | custom-call | tf_op jit(solution)/shard_map/pallas_call | solution.py:515
  81.2 1.2 %slice_bitcast_fusion = f32[9]{0:T(128)} fusion(f32[1,128]{1,0:T(1,128)} %get-tuple-element.5), kind=kLoop, calls=%fused_computation | loop fusion | bytes 72 | tf_op jit(solution)/shard_map/squeeze | solution.py:550
  82.4 1.6 %copy.10 = f32[1,32,1024]{2,1,0:T(8,128)} copy(f32[1,32,1024]{2,1,0:T(8,128)} %get-tuple-element.8) | data formatting | bytes 262144

commit v3 on v2

--- a/solution.py
+++ b/solution.py
@@ -94,7 +94,7 @@
         at += 2 * count
     small = np.arange(128)
     short = np.arange(32)
-    twist = np.zeros((96, 128))
+    twist = np.zeros((1024, 128))
     angle = 2 * np.pi / GRID * ((np.arange(1, 4)[:, None] * small[None, :]) % GRID)
     twist[0:3], twist[8:11] = np.cos(angle), np.sin(angle)
     angle = 2 * np.pi / GRID * ((short[:, None] * short[None, :]) % GRID)
@@ -144,7 +144,8 @@
     steps_ref, shift_ref, basis_hbm, grad_hbm, table_hbm, twist_hbm,
     out_ref, hess_ref,
     basis, grad, table, twist, counts,
-    s1, s2, s3, s4, s5, s6, r1, r2, r3, r4, r5, r6,
+    s1, s2, s3, s5, s6, r1, r2, r3, r5, r6,
+    pairs_out, pairs_in, spectra,
     mine, sum_a, sum_b,
     local_sem, send_sem, recv_sem, ready,
 ):
@@ -159,7 +160,7 @@
     loads = [
         pltpu.make_async_copy(source, target, local_sem.at[at])
         for at, (source, target) in enumerate(
-            ((basis_hbm, basis), (twist_hbm, twist), (table_hbm, table), (grad_hbm, grad))
+            ((basis_hbm, basis), (twist_hbm.at[pl.ds(0, 96)], twist), (table_hbm, table), (grad_hbm, grad))
         )
     ]
     for load in loads:
@@ -245,6 +246,65 @@
             device_id={"space": me},
             device_id_type=MESH,
         )
+
+    def coded(value):
+        top = jnp.maximum(jnp.max(jnp.abs(value), axis=0, keepdims=True), 1e-30)
+        level = jnp.ceil(256.0 * jnp.log2(top)).astype(jnp.int32) + 1
+        scale = jnp.exp2(15.0 - level.astype(f32) * (1.0 / 256.0))
+        return jnp.floor(value * scale + 0.5).astype(jnp.int32), level
+
+    def joined(high, low):
+        return (high << 16) | (low & 0xFFFF)
+
+    def parted(word):
+        return word >> 16, (word << 16) >> 16
+
+    def send_pair(first, second, at, to_seg):
+        first_code, first_level = coded(first)
+        second_code, second_level = coded(second)
+        pairs_out[at, :, 0:8, :] = joined(first_code, second_code).reshape(SPACE, 8, 128)
+        level = joined(first_level, second_level)
+        pairs_out[at, :, 8:9, :] = jnp.broadcast_to(level.reshape(1, 1, 128), (SPACE, 1, 128))
+
+        def step_to(step, carry):
+            peer = peer_in_space(step)
+            pltpu.make_async_remote_copy(
+                src_ref=pairs_out.at[at, peer],
+                dst_ref=pairs_in.at[at, me],
+                send_sem=send_sem.at[9 + at],
+                recv_sem=recv_sem.at[9 + at],
+                device_id={"seg": to_seg, "space": peer},
+                device_id_type=MESH,
+            ).start()
+            return carry
+
+        lax.fori_loop(0, SPACE, step_to, 0)
+
+    def pair_done(at):
+        return pltpu.make_async_remote_copy(
+            src_ref=pairs_out.at[at],
+            dst_ref=pairs_in.at[at],
+            send_sem=send_sem.at[9 + at],
+            recv_sem=recv_sem.at[9 + at],
+            device_id={"space": me},
+            device_id_type=MESH,
+        )
+
+    def received_pair(at):
+        codes = parted(pairs_in[at, :, 0:8, :])
+        levels = parted(pairs_in[at, :, 8:9, :])
+        return [
+            (code.astype(f32) * jnp.exp2(level.astype(f32) * (1.0 / 256.0) - 15.0)).reshape(256, 128)
+            for code, level in zip(codes, levels)
+        ]
+
+    def basis_spectra(at):
+        for index in (2 * at, 2 * at + 1):
+            if index == KRYLOV - 1:
+                spectra[index] = weight * s1[...]
+            else:
+                zero, rest = row_spectrum(basis[index].astype(f32))
+                spectra[index] = weight * jnp.concatenate([zero, rest], axis=0).T
 
     def row_spectrum(field):
         group = [field[:, 128 * at : 128 * at + 128] for at in range(8)]
@@ -321,6 +381,11 @@
             axis=0,
         )
         return const_left("M1", value)
+
+    pair_row = lax.broadcasted_iota(jnp.int32, (256, 128), 0)
+    pair_lane = lax.broadcasted_iota(jnp.int32, (256, 128), 1)
+    alone = (pair_row < 8) & (pair_row % 4 == 0) & (pair_lane < 32)
+    weight = jnp.where(alone, 1.0 / GRID, 2.0 / GRID).astype(f32)
 
     loads[0].wait()
     loads[1].wait()
@@ -339,6 +404,7 @@
     )
     count_copy.start()
     send(s1, r1, 0, 8, other)
+    basis_spectra(0)
 
     waves = [
         jnp.concatenate([twist[80 + at : 81 + at, :], twist[88 + at : 89 + at, :]], axis=1)
@@ -371,6 +437,7 @@
 
     s2[...] = columns_inverse(-deriv_x * state_im, deriv_x * state_re)
     send(s2, r2, 1, 8, other)
+    basis_spectra(1)
     loads[3].wait()
     part_y = grad[1].astype(f32) * grad_y
     part_x = -grad[0].astype(f32)
@@ -380,6 +447,7 @@
 
     rows_forward(term, s3)
     send(s3, r3, 2, 8, other)
+    basis_spectra(2)
     flat = basis[...].reshape(KRYLOV * ROWS, GRID)
     gram = lax.dot_general(flat, flat, (((1,), (1,)), ((), ())), preferred_element_type=f32)
     gram_row = lax.broadcasted_iota(jnp.int32, (256, 256), 0)
@@ -402,18 +470,15 @@
 
     toward_x = columns_inverse(-deriv_x * middle_im, deriv_x * middle_re)
     toward_y = columns_inverse(-deriv_y * middle_im, deriv_y * middle_re)
-    for peer in range(SPACE):
-        s4[16 * peer : 16 * peer + 8, :] = toward_x[8 * peer : 8 * peer + 8]
-        s4[16 * peer + 8 : 16 * peer + 16, :] = toward_y[8 * peer : 8 * peer + 8]
-    send(s4, r4, 3, 16, other)
+    send_pair(toward_x, toward_y, 0, other)
+    basis_spectra(3)
     offset = (freq_x * shift_ref[0] + freq_y * shift_ref[1]) & (GRID - 1)
     angle = (2.0 * math.pi / GRID) * offset.astype(f32)
     is_last = other == SEGS - 1
     cosine = jnp.where(is_last, jnp.cos(angle), 1.0)
     sine = jnp.where(is_last, jnp.sin(angle), 0.0)
-    arrival(s4, r4, 3, 512).wait_recv()
-    got_x = jnp.concatenate([r4[16 * peer : 16 * peer + 8, :] for peer in range(SPACE)], axis=0)
-    got_y = jnp.concatenate([r4[16 * peer + 8 : 16 * peer + 16, :] for peer in range(SPACE)], axis=0)
+    pair_done(0).wait_recv()
+    got_x, got_y = received_pair(0)
     term = -(grad[2].astype(f32) * rows_inverse(got_x) + grad[3].astype(f32) * rows_inverse(got_y))
 
     rows_forward(term, s5)
@@ -429,16 +494,16 @@
     pl.semaphore_wait(ready, 1)
     send(s6, r6, 5, 8, after)
     arrival(s6, r6, 5, 256).wait_recv()
-    wrapped = rows_inverse(r6[...]) - start
+    flow = r6[...]
 
     def folded(value):
-        total = value[:, :128]
-        for at in range(1, 8):
-            total = total + value[:, 128 * at : 128 * at + 128]
+        total = value[:8]
+        for at in range(1, 32):
+            total = total + value[8 * at : 8 * at + 8]
         return jnp.sum(total, axis=0, keepdims=True)
 
-    lines = [folded(wrapped * basis[at].astype(f32)) for at in range(KRYLOV)]
-    lines.append(folded(wrapped * wrapped))
+    lines = [folded(flow * spectra[at]) for at in range(KRYLOV)]
+    lines.append(folded(flow * flow * weight))
     lines.append(jnp.zeros((7, 128), f32))
     sums = jnp.sum(jnp.concatenate(lines, axis=0), axis=1, keepdims=True)
     spot_row = lax.broadcasted_iota(jnp.int32, (16, 128), 0)
@@ -460,7 +525,7 @@
             return carry
 
         lax.fori_loop(0, count - 1, step_to, 0)
-        done = pltpu.make_async_remote_copy(
+        return pltpu.make_async_remote_copy(
             src_ref=target.at[pl.ds(0, count - 1)],
             dst_ref=target.at[pl.ds(0, count - 1)],
             send_sem=send_sem.at[6 + at],
@@ -468,22 +533,26 @@
             device_id={"seg": other},
             device_id_type=MESH,
         )
-        done.wait_recv()
-        return done, jnp.sum(target[...], axis=0)
 
     mine[0] = line
-    sent_a, line = spread(sum_a, peer_in_column, place, COLUMN, 0)
-    mine[1] = line
-    sent_b, line = spread(sum_b, peer_in_plane, 8 * chip_x + chip_z, PLANE, 1)
-    line = line * (1.0 / (SEGS * GRID * GRID))
+    sent_a = spread(sum_a, peer_in_column, place, COLUMN, 0)
+    wrapped = rows_inverse(flow) - start
+    sent_a.wait_recv()
+    mine[1] = jnp.sum(sum_a[...], axis=0)
+    sent_b = spread(sum_b, peer_in_plane, 8 * chip_x + chip_z, PLANE, 1)
+    sent_b.wait_recv()
+    line = jnp.sum(sum_b[...], axis=0) * (1.0 / (SEGS * GRID * GRID))
 
     lanes = lax.broadcasted_iota(jnp.int32, (1, 128), 1)
 
-    def lane_of(at):
-        return jnp.sum(jnp.where(lanes == at, line, 0.0), axis=1, keepdims=True)
-
-    coeffs = [lane_of(at) for at in range(KRYLOV)]
-    norm_sq = lane_of(KRYLOV)
+    def lane_of(*signed_places):
+        value = jnp.zeros((1, 128), f32)
+        for sign, at in signed_places:
+            value = value + jnp.where(lanes == at, sign * line, 0.0)
+        return jnp.sum(value, axis=1, keepdims=True)
+
+    coeffs = [lane_of((1.0, at), (-1.0, 16 + 8 * at + 7)) for at in range(KRYLOV)]
+    norm_sq = lane_of((1.0, KRYLOV), (-2.0, KRYLOV - 1), (1.0, 79))
     left = jnp.zeros((1, 128), f32)
     right = jnp.zeros((1, 128), f32)
     for at in range(KRYLOV):
@@ -492,17 +561,21 @@
         norm_sq = norm_sq - 2.0 * coeffs[at] * coeffs[at]
     norm_sq = norm_sq + jnp.sum(left * right * line, axis=1, keepdims=True)
     norm = jnp.sqrt(norm_sq)
-    hess_ref[...] = jnp.where(lanes == KRYLOV, norm, line)
+    column = jnp.where(lanes == KRYLOV, norm, 0.0)
+    for at in range(KRYLOV):
+        column = jnp.where(lanes == at, coeffs[at], column)
+    hess_ref[...] = column
     inverse = 1.0 / norm
     remainder = wrapped
     for at in range(KRYLOV):
         remainder = remainder - coeffs[at] * basis[at].astype(f32)
     out_ref[0] = remainder * inverse
 
-    for source, at, rows in ((s1, 0, 256), (s2, 1, 256), (s3, 2, 256), (s4, 3, 512), (s5, 4, 256), (s6, 5, 256)):
+    for source, at, rows in ((s1, 0, 256), (s2, 1, 256), (s3, 2, 256), (s5, 4, 256), (s6, 5, 256)):
         arrival(source, source, at, rows).wait_send()
     sent_a.wait_send()
     sent_b.wait_send()
+    pair_done(0).wait_send()
     count_copy.wait_send()
 
 
@@ -511,7 +584,6 @@
     scalars = pl.BlockSpec(memory_space=pltpu.SMEM)
     f32, bf16 = jnp.float32, jnp.bfloat16
     tile = pltpu.VMEM((256, 128), f32)
-    wide = pltpu.VMEM((512, 128), f32)
     new_vector, line = pl.pallas_call(
         kernel,
         out_shape=(
@@ -524,20 +596,23 @@
             pltpu.VMEM((KRYLOV, ROWS, GRID), bf16),
             pltpu.VMEM((4, ROWS, GRID), bf16),
             pltpu.VMEM(TABLE.shape, bf16),
-            pltpu.VMEM(TWIST.shape, f32),
+            pltpu.VMEM((96, 128), f32),
             pltpu.VMEM((2, 1, 128), jnp.int32),
-            tile, tile, tile, wide, tile, tile,
-            tile, tile, tile, wide, tile, tile,
+            tile, tile, tile, tile, tile,
+            tile, tile, tile, tile, tile,
+            pltpu.VMEM((1, SPACE, 9, 128), jnp.int32),
+            pltpu.VMEM((1, SPACE, 9, 128), jnp.int32),
+            pltpu.VMEM((KRYLOV, 256, 128), f32),
             pltpu.VMEM((2, 1, 128), f32),
             pltpu.VMEM((COLUMN, 1, 128), f32),
             pltpu.VMEM((PLANE, 1, 128), f32),
             pltpu.SemaphoreType.DMA((4,)),
-            pltpu.SemaphoreType.DMA((9,)),
-            pltpu.SemaphoreType.DMA((9,)),
+            pltpu.SemaphoreType.DMA((10,)),
+            pltpu.SemaphoreType.DMA((10,)),
             pltpu.SemaphoreType.REGULAR,
         ],
         compiler_params=pltpu.CompilerParams(
-            collective_id=0, has_side_effects=True, vmem_limit_bytes=62 * 1024 * 1024
+            collective_id=0, has_side_effects=True, vmem_limit_bytes=54976 * 1024
         ),
     )(
         step_counts,

time: 84.1 us -> 80 us (0.951)
  Pallas kernels: 79.9 us -> 76.8 us
  local copies, waits for them, and re-layouts: 2.74 us -> 1.82 us
    pallas_call x1, Pallas kernels: 79.9 us -> 76.8 us  [per_device(): pl.pallas_call(kernel, out_shape=(jax.ShapeDtypeStruct((1, ROWS, GRID), f...]
where the time goes in v3:
time: 80 us; the launch traced here: 79.9 us
  Pallas kernels  76.8 us (96%)
  local copies, waits for them, and re-layouts  1.82 us (2%)
  between operations  1.29 us (2%)
    pallas_call x1, Pallas kernels, per_device(): pl.pallas_call(kernel, out_shape=(jax.ShapeDtypeStruct((1, ROWS, GRID), f...  76.8 us

profile of v3, /device:TPU:1, one launch (start us, length us, event | category | flops | bytes accessed | tf_op | source)
XLA Modules:
  0.0 79.9 jit_solution(2829280485242665591)
XLA Ops:
  1.3 0.0 copy-start
  1.3 0.6 copy-done
  1.9 76.8 %shard_map.77 = (f32[1,32,1024]{2,1,0:T(8,128)S(1)}, f32[1,128]{1,0:T(1,128)S(1)}) custom-call(s32[1]{0:T(128)S(6)} %copy.9.steps_ref, s32[2]{0:T(128)S(1)} %copy-done, bf16[8,32,1024]{2,1,0:T(8,128)(2,1)} %bitcast.4, bf16[4,32,1024]{2,1,0:T(8,128)(2,1)} %bitcast.5, bf16[5248,256]{1,0:T(8,128)(2,1)} %constant.4.clone.table_hbm, ...), custom_call_target="tpu_custom_call" | custom-call | tf_op jit(solution)/shard_map/pallas_call | solution.py:587
  78.7 0.5 slice_bitcast_fusion
  79.2 0.7 copy.10
Async XLA Ops:
  1.3 0.7 copy-start

commit v4 on v3

--- a/solution.py
+++ b/solution.py
@@ -27,16 +27,13 @@
     short = np.arange(32)
 
     def by_owner(real, imag):
-        parts = [part.reshape(part.shape[0], 32, 4) for part in (real, imag)]
-        return np.stack(parts, axis=2).reshape(real.shape[0], 256)
+        return np.concatenate([real, imag], axis=1)
 
     def owner_rows(real, imag):
-        parts = [part.reshape(32, 4, -1) for part in (real, imag)]
-        return np.stack(parts, axis=1).reshape(256, -1)
+        return np.concatenate([real, imag], axis=0)
 
     def swapped(table):
-        parts = table.reshape(32, 2, 4, 256)
-        return np.stack([parts[:, 1], -parts[:, 0]], axis=1).reshape(256, 256)
+        return np.concatenate([table[128:], -table[:128]], axis=0)
 
     angle = 2 * np.pi / 256 * ((full[:, None] * small[None, :]) % 256)
     real, imag = np.cos(angle), -np.sin(angle)
@@ -55,21 +52,21 @@
     tabs["D1"] = swapped(tabs["B1"])
     angle = 2 * np.pi / 32 * ((short[:, None] * short[None, :]) % 32)
     cos, sin = np.cos(angle), np.sin(angle)
-    table = np.zeros((2, 5, 32, 32, 2, 4))
+    table = np.zeros((2, 5, 32, 2, 32, 4))
     for low in range(4):
-        table[0, low, :, :, 0, low] = cos
-        table[0, low, :, :, 1, low] = sin
-        table[1, low, :, :, 0, low] = -sin
-        table[1, low, :, :, 1, low] = cos
-    table[0, 4, :, :, 1, 0] = cos
-    table[1, 4, :, :, 1, 0] = -sin
+        table[0, low, :, 0, :, low] = cos
+        table[0, low, :, 1, :, low] = sin
+        table[1, low, :, 0, :, low] = -sin
+        table[1, low, :, 1, :, low] = cos
+    table[0, 4, :, 1, :, 0] = cos
+    table[1, 4, :, 1, :, 0] = -sin
     tabs["L1"] = table.reshape(320, 256)
-    table = np.zeros((32, 2, 4, 2, 4, 32))
+    table = np.zeros((2, 32, 4, 2, 4, 32))
     for low in range(4):
-        table[:, 0, low, 0, low, :] = cos
-        table[:, 0, low, 1, low, :] = -sin
-        table[:, 1, low, 0, low, :] = sin
-        table[:, 1, low, 1, low, :] = cos
+        table[0, :, low, 0, low, :] = cos
+        table[0, :, low, 1, low, :] = -sin
+        table[1, :, low, 0, low, :] = sin
+        table[1, :, low, 1, low, :] = cos
     tabs["M1"] = table.reshape(256, 256) / GRID
     for name, sign in (("L2", 1.0), ("M2", -1.0)):
         table = np.zeros((2, 4, 32, 2, 4, 32))
@@ -103,8 +100,7 @@
     for slot in range(4):
         freq = 4 * small if slot == 0 else slot + 8 * small
         freq = np.where(freq < GRID // 2, freq, freq - GRID) * (8.0 / GRID)
-        lanes = np.stack([freq.reshape(32, 4)] * 2, axis=1).reshape(256)
-        twist[80 + slot], twist[88 + slot] = lanes[:128], lanes[128:]
+        twist[80 + slot] = freq
     return offsets, np.concatenate(parts, 0), twist.astype(np.float32)
 
 
@@ -144,8 +140,7 @@
     steps_ref, shift_ref, basis_hbm, grad_hbm, table_hbm, twist_hbm,
     out_ref, hess_ref,
     basis, grad, table, twist, counts,
-    s1, s2, s3, s5, s6, r1, r2, r3, r5, r6,
-    pairs_out, pairs_in, spectra,
+    ones_out, ones_in, pair_out, pair_in, spectra,
     mine, sum_a, sum_b,
     local_sem, send_sem, recv_sem, ready,
 ):
@@ -216,20 +211,39 @@
         return both[:, :128] + both[:, 128:] + dot(table_low, high)
 
     def const_right(value, name):
-        count = value.shape[0]
         high, low = halves(value)
         table_high, table_low = const(name)
-        both = dot(jnp.concatenate([high, low], axis=0), table_high)
-        return both[:count] + both[count:] + dot(high, table_low)
-
-    def send(source, target, at, rows, to_seg):
+        return dot(
+            jnp.concatenate([high, high, low], axis=1),
+            jnp.concatenate([table_high, table_low, table_high], axis=0),
+        )
+
+    def coded(field):
+        real, imag = field[:128], field[128:]
+        top = jnp.max(jnp.maximum(jnp.abs(real), jnp.abs(imag)), axis=0, keepdims=True)
+        level = jnp.ceil(256.0 * jnp.log2(jnp.maximum(top, 1e-30))).astype(jnp.int32) + 1
+        scale = jnp.exp2(15.0 - level.astype(f32) * (1.0 / 256.0))
+        high = jnp.floor(real * scale + 0.5).astype(jnp.int32)
+        low = jnp.floor(imag * scale + 0.5).astype(jnp.int32)
+        return (high << 16) | (low & 0xFFFF), level
+
+    def pack(fields, source, at):
+        count = len(fields)
+        for which, field in enumerate(fields):
+            words, level = coded(field)
+            for peer in range(SPACE):
+                source[at, peer, 4 * which : 4 * which + 4, :] = words[4 * peer : 4 * peer + 4]
+            row = 4 * count + which
+            source[at, :, row : row + 1, :] = jnp.broadcast_to(level.reshape(1, 1, 128), (SPACE, 1, 128))
+
+    def send(source, target, at, sem, to_seg):
         def step_to(step, carry):
             peer = peer_in_space(step)
             pltpu.make_async_remote_copy(
-                src_ref=source.at[pl.ds(pl.multiple_of(peer * rows, 8), rows)],
-                dst_ref=target.at[pl.ds(pl.multiple_of(me * rows, 8), rows)],
-                send_sem=send_sem.at[at],
-                recv_sem=recv_sem.at[at],
+                src_ref=source.at[at, peer],
+                dst_ref=target.at[at, me],
+                send_sem=send_sem.at[sem],
+                recv_sem=recv_sem.at[sem],
                 device_id={"seg": to_seg, "space": peer},
                 device_id_type=MESH,
             ).start()
@@ -237,71 +251,43 @@
 
         lax.fori_loop(0, SPACE, step_to, 0)
 
-    def arrival(source, target, at, rows):
+    def arrival(source, target, at, sem):
         return pltpu.make_async_remote_copy(
-            src_ref=source.at[pl.ds(0, rows)],
-            dst_ref=target.at[pl.ds(0, rows)],
-            send_sem=send_sem.at[at],
-            recv_sem=recv_sem.at[at],
+            src_ref=source.at[at],
+            dst_ref=target.at[at],
+            send_sem=send_sem.at[sem],
+            recv_sem=recv_sem.at[sem],
             device_id={"space": me},
             device_id_type=MESH,
         )
 
-    def coded(value):
-        top = jnp.maximum(jnp.max(jnp.abs(value), axis=0, keepdims=True), 1e-30)
-        level = jnp.ceil(256.0 * jnp.log2(top)).astype(jnp.int32) + 1
-        scale = jnp.exp2(15.0 - level.astype(f32) * (1.0 / 256.0))
-        return jnp.floor(value * scale + 0.5).astype(jnp.int32), level
-
-    def joined(high, low):
-        return (high << 16) | (low & 0xFFFF)
-
-    def parted(word):
-        return word >> 16, (word << 16) >> 16
-
-    def send_pair(first, second, at, to_seg):
-        first_code, first_level = coded(first)
-        second_code, second_level = coded(second)
-        pairs_out[at, :, 0:8, :] = joined(first_code, second_code).reshape(SPACE, 8, 128)
-        level = joined(first_level, second_level)
-        pairs_out[at, :, 8:9, :] = jnp.broadcast_to(level.reshape(1, 1, 128), (SPACE, 1, 128))
-
-        def step_to(step, carry):
-            peer = peer_in_space(step)
-            pltpu.make_async_remote_copy(
-                src_ref=pairs_out.at[at, peer],
-                dst_ref=pairs_in.at[at, me],
-                send_sem=send_sem.at[9 + at],
-                recv_sem=recv_sem.at[9 + at],
-                device_id={"seg": to_seg, "space": peer},
-                device_id_type=MESH,
-            ).start()
-            return carry
-
-        lax.fori_loop(0, SPACE, step_to, 0)
-
-    def pair_done(at):
-        return pltpu.make_async_remote_copy(
-            src_ref=pairs_out.at[at],
-            dst_ref=pairs_in.at[at],
-            send_sem=send_sem.at[9 + at],
-            recv_sem=recv_sem.at[9 + at],
-            device_id={"space": me},
-            device_id_type=MESH,
-        )
-
-    def received_pair(at):
-        codes = parted(pairs_in[at, :, 0:8, :])
-        levels = parted(pairs_in[at, :, 8:9, :])
-        return [
-            (code.astype(f32) * jnp.exp2(level.astype(f32) * (1.0 / 256.0) - 15.0)).reshape(256, 128)
-            for code, level in zip(codes, levels)
-        ]
+    def received(target, at, count):
+        fields = []
+        for which in range(count):
+            rows = [target[at, peer, 4 * which : 4 * which + 4, :] for peer in range(SPACE)]
+            words = jnp.concatenate(rows, axis=0)
+            row = 4 * count + which
+            levels = [
+                jnp.broadcast_to(target[at, peer, row : row + 1, :], (4, 128)) for peer in range(SPACE)
+            ]
+            scale = jnp.exp2(jnp.concatenate(levels, axis=0).astype(f32) * (1.0 / 256.0) - 15.0)
+            real = (words >> 16).astype(f32) * scale
+            imag = ((words << 16) >> 16).astype(f32) * scale
+            fields.append(jnp.concatenate([real, imag], axis=0))
+        return fields
+
+    def send_one(field, at, to_seg):
+        pack([field], ones_out, at)
+        send(ones_out, ones_in, at, at, to_seg)
+
+    def receive_one(at):
+        arrival(ones_out, ones_in, at, at).wait_recv()
+        return received(ones_in, at, 1)[0]
 
     def basis_spectra(at):
         for index in (2 * at, 2 * at + 1):
             if index == KRYLOV - 1:
-                spectra[index] = weight * s1[...]
+                spectra[index] = weight * start_spectrum
             else:
                 zero, rest = row_spectrum(basis[index].astype(f32))
                 spectra[index] = weight * jnp.concatenate([zero, rest], axis=0).T
@@ -345,13 +331,12 @@
         pieces += [sums[at] - differences[at] for at in range(4)]
         return jnp.concatenate(pieces, axis=1)
 
-    def rows_forward(field, target):
+    def rows_forward(field):
         zero, rest = row_spectrum(field)
-        target[...] = jnp.concatenate([zero, rest], axis=0).T
-        return zero, rest
-
-    def rows_inverse(received):
-        turned = received.T
+        return jnp.concatenate([zero, rest], axis=0).T
+
+    def rows_inverse(spectrum):
+        turned = spectrum.T
         return row_field(const_right(turned[:32], "B0"), const_right(turned[32:], "B1"))
 
     def stacked(value):
@@ -384,15 +369,18 @@
 
     pair_row = lax.broadcasted_iota(jnp.int32, (256, 128), 0)
     pair_lane = lax.broadcasted_iota(jnp.int32, (256, 128), 1)
-    alone = (pair_row < 8) & (pair_row % 4 == 0) & (pair_lane < 32)
+    alone = (pair_row % 128 == 0) & (pair_lane < 32)
     weight = jnp.where(alone, 1.0 / GRID, 2.0 / GRID).astype(f32)
 
     loads[0].wait()
     loads[1].wait()
     loads[2].wait()
     start = basis[KRYLOV - 1].astype(f32)
-    zero, rest = rows_forward(start, s1)
+    zero, rest = row_spectrum(start)
+    start_spectrum = jnp.concatenate([zero, rest], axis=0).T
+    pack([start_spectrum], ones_out, 0)
     pl.semaphore_wait(barrier, SPACE + PLANE - 1)
+    send(ones_out, ones_in, 0, 0, other)
     counts[0] = jnp.full((1, 128), steps_ref[0], jnp.int32)
     count_copy = pltpu.make_async_remote_copy(
         src_ref=counts.at[0],
@@ -403,11 +391,10 @@
         device_id_type=MESH,
     )
     count_copy.start()
-    send(s1, r1, 0, 8, other)
     basis_spectra(0)
 
     waves = [
-        jnp.concatenate([twist[80 + at : 81 + at, :], twist[88 + at : 89 + at, :]], axis=1)
+        jnp.concatenate([twist[80 + at : 81 + at, :]] * 2, axis=1)
         for at in range(4)
     ]
     lifted = jnp.concatenate([rest[32 * at : 32 * at + 32] * waves[at + 1] for at in range(3)], axis=0)
@@ -431,22 +418,18 @@
     phi_one = step_size * phi_one
     phi_two = step_size * phi_two
 
-    done = arrival(s1, r1, 0, 256)
-    done.wait_recv()
-    state_re, state_im = columns_forward(r1[...])
-
-    s2[...] = columns_inverse(-deriv_x * state_im, deriv_x * state_re)
-    send(s2, r2, 1, 8, other)
+    state_re, state_im = columns_forward(receive_one(0))
+
+    send_one(columns_inverse(-deriv_x * state_im, deriv_x * state_re), 1, other)
     basis_spectra(1)
     loads[3].wait()
     part_y = grad[1].astype(f32) * grad_y
     part_x = -grad[0].astype(f32)
-    arrival(s2, r2, 1, 256).wait_recv()
+    slope = receive_one(1)
     pl.semaphore_signal(ready, inc=1, device_id={"seg": before}, device_id_type=MESH)
-    term = part_x * rows_inverse(r2[...]) - part_y
-
-    rows_forward(term, s3)
-    send(s3, r3, 2, 8, other)
+    term = part_x * rows_inverse(slope) - part_y
+
+    send_one(rows_forward(term), 2, other)
     basis_spectra(2)
     flat = basis[...].reshape(KRYLOV * ROWS, GRID)
     gram = lax.dot_general(flat, flat, (((1,), (1,)), ((), ())), preferred_element_type=f32)
@@ -463,38 +446,35 @@
         part = jnp.sum(jnp.where(gram_lane[:8] // 32 == at, gram, 0.0), axis=1, keepdims=True)
         gram_sums = gram_sums + jnp.where(spot_lane == 16 + 8 * spot_row + at, part, 0.0)
     gram_sums = jnp.sum(gram_sums, axis=0, keepdims=True)
-    arrival(s3, r3, 2, 256).wait_recv()
-    term_re, term_im = columns_forward(r3[...])
+    term_re, term_im = columns_forward(receive_one(2))
     middle_re = decay * state_re + phi_one * term_re
     middle_im = decay * state_im + phi_one * term_im
 
     toward_x = columns_inverse(-deriv_x * middle_im, deriv_x * middle_re)
     toward_y = columns_inverse(-deriv_y * middle_im, deriv_y * middle_re)
-    send_pair(toward_x, toward_y, 0, other)
+    pack([toward_x, toward_y], pair_out, 0)
+    send(pair_out, pair_in, 0, 5, other)
     basis_spectra(3)
     offset = (freq_x * shift_ref[0] + freq_y * shift_ref[1]) & (GRID - 1)
     angle = (2.0 * math.pi / GRID) * offset.astype(f32)
     is_last = other == SEGS - 1
     cosine = jnp.where(is_last, jnp.cos(angle), 1.0)
     sine = jnp.where(is_last, jnp.sin(angle), 0.0)
-    pair_done(0).wait_recv()
-    got_x, got_y = received_pair(0)
+    arrival(pair_out, pair_in, 0, 5).wait_recv()
+    got_x, got_y = received(pair_in, 0, 2)
     term = -(grad[2].astype(f32) * rows_inverse(got_x) + grad[3].astype(f32) * rows_inverse(got_y))
 
-    rows_forward(term, s5)
-    send(s5, r5, 4, 8, other)
+    send_one(rows_forward(term), 3, other)
     kept_re = middle_re - phi_two * term_re
     kept_im = middle_im - phi_two * term_im
-    arrival(s5, r5, 4, 256).wait_recv()
-    term_re, term_im = columns_forward(r5[...])
+    term_re, term_im = columns_forward(receive_one(3))
     state_re = kept_re + phi_two * term_re
     state_im = kept_im + phi_two * term_im
 
-    s6[...] = columns_inverse(cosine * state_re + sine * state_im, cosine * state_im - sine * state_re)
+    flow = columns_inverse(cosine * state_re + sine * state_im, cosine * state_im - sine * state_re)
     pl.semaphore_wait(ready, 1)
-    send(s6, r6, 5, 8, after)
-    arrival(s6, r6, 5, 256).wait_recv()
-    flow = r6[...]
+    send_one(flow, 4, after)
+    flow = receive_one(4)
 
     def folded(value):
         total = value[:8]
@@ -571,11 +551,11 @@
         remainder = remainder - coeffs[at] * basis[at].astype(f32)
     out_ref[0] = remainder * inverse
 
-    for source, at, rows in ((s1, 0, 256), (s2, 1, 256), (s3, 2, 256), (s5, 4, 256), (s6, 5, 256)):
-        arrival(source, source, at, rows).wait_send()
+    for at in range(5):
+        arrival(ones_out, ones_in, at, at).wait_send()
+    arrival(pair_out, pair_in, 0, 5).wait_send()
     sent_a.wait_send()
     sent_b.wait_send()
-    pair_done(0).wait_send()
     count_copy.wait_send()
 
 
@@ -583,7 +563,6 @@
     any_space = pl.BlockSpec(memory_space=pl.ANY)
     scalars = pl.BlockSpec(memory_space=pltpu.SMEM)
     f32, bf16 = jnp.float32, jnp.bfloat16
-    tile = pltpu.VMEM((256, 128), f32)
     new_vector, line = pl.pallas_call(
         kernel,
         out_shape=(
@@ -598,17 +577,17 @@
             pltpu.VMEM(TABLE.shape, bf16),
             pltpu.VMEM((96, 128), f32),
             pltpu.VMEM((2, 1, 128), jnp.int32),
-            tile, tile, tile, tile, tile,
-            tile, tile, tile, tile, tile,
-            pltpu.VMEM((1, SPACE, 9, 128), jnp.int32),
-            pltpu.VMEM((1, SPACE, 9, 128), jnp.int32),
+            pltpu.VMEM((5, SPACE, 5, 128), jnp.int32),
+            pltpu.VMEM((5, SPACE, 5, 128), jnp.int32),
+            pltpu.VMEM((1, SPACE, 10, 128), jnp.int32),
+            pltpu.VMEM((1, SPACE, 10, 128), jnp.int32),
             pltpu.VMEM((KRYLOV, 256, 128), f32),
             pltpu.VMEM((2, 1, 128), f32),
             pltpu.VMEM((COLUMN, 1, 128), f32),
             pltpu.VMEM((PLANE, 1, 128), f32),
             pltpu.SemaphoreType.DMA((4,)),
-            pltpu.SemaphoreType.DMA((10,)),
-            pltpu.SemaphoreType.DMA((10,)),
+            pltpu.SemaphoreType.DMA((9,)),
+            pltpu.SemaphoreType.DMA((9,)),
             pltpu.SemaphoreType.REGULAR,
         ],
         compiler_params=pltpu.CompilerParams(

time: 80 us -> 76.3 us (0.954)
  Pallas kernels: 76.8 us -> 73.1 us
    pallas_call x1, Pallas kernels: 76.8 us -> 73.1 us  [per_device(): pl.pallas_call(kernel, out_shape=(jax.ShapeDtypeStruct((1, ROWS, GRID), f...]
where the time goes in v4:
time: 76.3 us; the launch traced here: 76.2 us
  Pallas kernels  73.1 us (96%)
  local copies, waits for them, and re-layouts  1.82 us (2%)
  between operations  1.29 us (2%)
    pallas_call x1, Pallas kernels, per_device(): pl.pallas_call(kernel, out_shape=(jax.ShapeDtypeStruct((1, ROWS, GRID), f...  73.1 us

profile of v4, /device:TPU:1, one launch (start us, length us, event | category | flops | bytes accessed | tf_op | source)
XLA Modules:
  0.0 76.2 jit_solution(5798983630249745153)
XLA Ops:
  1.3 0.0 copy-start
  1.3 0.6 copy-done
  1.9 73.1 %shard_map.77 = (f32[1,32,1024]{2,1,0:T(8,128)S(1)}, f32[1,128]{1,0:T(1,128)S(1)}) custom-call(s32[1]{0:T(128)S(6)} %copy.9.steps_ref, s32[2]{0:T(128)S(1)} %copy-done, bf16[8,32,1024]{2,1,0:T(8,128)(2,1)} %bitcast.4, bf16[4,32,1024]{2,1,0:T(8,128)(2,1)} %bitcast.5, bf16[5248,256]{1,0:T(8,128)(2,1)} %constant.4.clone.table_hbm, ...), custom_call_target="tpu_custom_call" | custom-call | tf_op jit(solution)/shard_map/pallas_call | solution.py:566
  75.0 0.5 slice_bitcast_fusion
  75.5 0.7 copy.10
Async XLA Ops:
  1.3 0.7 copy-start

commit v5 on v4

--- a/solution.py
+++ b/solution.py
@@ -142,7 +142,7 @@
     basis, grad, table, twist, counts,
     ones_out, ones_in, pair_out, pair_in, spectra,
     mine, sum_a, sum_b,
-    local_sem, send_sem, recv_sem, ready,
+    local_sem, send_sem, recv_sem, ready, plane,
 ):
     seg = lax.axis_index("seg")
     me = lax.axis_index("space")
@@ -158,9 +158,6 @@
             ((basis_hbm, basis), (twist_hbm.at[pl.ds(0, 96)], twist), (table_hbm, table), (grad_hbm, grad))
         )
     ]
-    for load in loads:
-        load.start()
-
     before = lax.rem(seg + SEGS - 1, SEGS)
     before = before + 2 - 4 * (lax.rem(before, 4) // 2)
     after = lax.rem(other + 1, SEGS)
@@ -171,34 +168,50 @@
         away = (step + 1) // 2
         return lax.rem(size + size // 2 + away * (1 - 2 * lax.rem(step, 2)), size)
 
-    def peer_in_space(step):
-        inner = lax.rem(step, 4)
-        chip_y = lax.rem(column_y + far_first(step // 4, 8), 8)
-        peer_core = lax.rem(core + 1 + lax.rem(inner, 2), 2)
-        return 16 * (inner // 2) + 2 * chip_y + peer_core
-
-    def peer_in_plane(step):
-        peer_z = lax.rem(chip_z + far_first(step // 4, 8), 8)
-        peer_x = lax.rem(chip_x + far_first(lax.rem(step, 4), 4), 4)
-        return {"seg": 4 * peer_x + lax.rem(peer_z, 4), "space": 16 * (peer_z // 4) + place}
-
-    def peer_in_column(step):
-        chip_y = lax.rem(column_y + far_first(step // 2, 8), 8)
-        peer_core = lax.rem(core + 1 + lax.rem(step, 2), 2)
-        return {"space": 16 * half + 2 * chip_y + peer_core}
+    def peers_in_space(step):
+        chip_y = 2 * lax.rem(column_y + far_first(step, 8), 8)
+        return [16 * upper + chip_y + peer_core for upper in (0, 1) for peer_core in (1 - core, core)]
+
+    def peers_in_plane(step):
+        peer_z = lax.rem(chip_z + far_first(step, 8), 8)
+        inner, upper = lax.rem(peer_z, 4), 16 * (peer_z // 4) + place
+        return [
+            {"seg": 4 * lax.rem(chip_x + away, 4) + inner, "space": upper} for away in (2, 1, 3, 0)
+        ]
+
+    def peers_in_column(step):
+        chip_y = 16 * half + 2 * lax.rem(column_y + far_first(step, 8), 8)
+        return [{"space": chip_y + peer_core} for peer_core in (1 - core, core)]
 
     def greet_space(step, carry):
-        pl.semaphore_signal(
-            barrier, inc=1, device_id={"seg": other, "space": peer_in_space(step)}, device_id_type=MESH
-        )
+        for peer in peers_in_space(step):
+            pl.semaphore_signal(
+                barrier, inc=1, device_id={"seg": other, "space": peer}, device_id_type=MESH
+            )
         return carry
 
-    def greet_plane(step, carry):
-        pl.semaphore_signal(barrier, inc=1, device_id=peer_in_plane(step), device_id_type=MESH)
+    def line_x(step):
+        return {"seg": 4 * lax.rem(chip_x + far_first(step, 4), 4) + lax.rem(seg, 4)}
+
+    def greet_x(step, carry):
+        pl.semaphore_signal(barrier, inc=1, device_id=line_x(step), device_id_type=MESH)
         return carry
 
-    lax.fori_loop(0, SPACE, greet_space, 0)
-    lax.fori_loop(0, PLANE - 1, greet_plane, 0)
+    def greet_z(step, carry):
+        peer_z = lax.rem(chip_z + far_first(step, 8), 8)
+        peer = {"seg": 4 * chip_x + lax.rem(peer_z, 4), "space": 16 * (peer_z // 4) + place}
+        pl.semaphore_signal(barrier, inc=1, device_id=peer, device_id_type=MESH)
+        return carry
+
+    def tell_x(step, carry):
+        pl.semaphore_signal(plane, inc=1, device_id=line_x(step), device_id_type=MESH)
+        return carry
+
+    lax.fori_loop(0, SPACE // 4, greet_space, 0)
+    lax.fori_loop(0, 7, greet_z, 0)
+    lax.fori_loop(0, 3, greet_x, 0)
+    for load in loads:
+        load.start()
 
     def const(name):
         at, count = OFFSETS[name]
@@ -238,18 +251,18 @@
 
     def send(source, target, at, sem, to_seg):
         def step_to(step, carry):
-            peer = peer_in_space(step)
-            pltpu.make_async_remote_copy(
-                src_ref=source.at[at, peer],
-                dst_ref=target.at[at, me],
-                send_sem=send_sem.at[sem],
-                recv_sem=recv_sem.at[sem],
-                device_id={"seg": to_seg, "space": peer},
-                device_id_type=MESH,
-            ).start()
+            for peer in peers_in_space(step):
+                pltpu.make_async_remote_copy(
+                    src_ref=source.at[at, peer],
+                    dst_ref=target.at[at, me],
+                    send_sem=send_sem.at[sem],
+                    recv_sem=recv_sem.at[sem],
+                    device_id={"seg": to_seg, "space": peer},
+                    device_id_type=MESH,
+                ).start()
             return carry
 
-        lax.fori_loop(0, SPACE, step_to, 0)
+        lax.fori_loop(0, SPACE // 4, step_to, 0)
 
     def arrival(source, target, at, sem):
         return pltpu.make_async_remote_copy(
@@ -379,8 +392,9 @@
     zero, rest = row_spectrum(start)
     start_spectrum = jnp.concatenate([zero, rest], axis=0).T
     pack([start_spectrum], ones_out, 0)
-    pl.semaphore_wait(barrier, SPACE + PLANE - 1)
+    pl.semaphore_wait(barrier, SPACE + 10)
     send(ones_out, ones_in, 0, 0, other)
+    lax.fori_loop(0, 3, tell_x, 0)
     counts[0] = jnp.full((1, 128), steps_ref[0], jnp.int32)
     count_copy = pltpu.make_async_remote_copy(
         src_ref=counts.at[0],
@@ -426,6 +440,7 @@
     part_y = grad[1].astype(f32) * grad_y
     part_x = -grad[0].astype(f32)
     slope = receive_one(1)
+    pl.semaphore_wait(plane, 3)
     pl.semaphore_signal(ready, inc=1, device_id={"seg": before}, device_id_type=MESH)
     term = part_x * rows_inverse(slope) - part_y
 
@@ -490,21 +505,26 @@
     spot_lane = lax.broadcasted_iota(jnp.int32, (16, 128), 1)
     line = jnp.sum(jnp.where(spot_row == spot_lane, sums, 0.0), axis=0, keepdims=True) + gram_sums
 
-    def spread(target, peer_of, own, count, at):
+    def spread(target, peers_of, own, count, at):
         target[own] = mine[at]
 
+        def send_to(peers):
+            for peer in peers:
+                pltpu.make_async_remote_copy(
+                    src_ref=mine.at[at],
+                    dst_ref=target.at[own],
+                    send_sem=send_sem.at[6 + at],
+                    recv_sem=recv_sem.at[6 + at],
+                    device_id=peer,
+                    device_id_type=MESH,
+                ).start()
+
         def step_to(step, carry):
-            pltpu.make_async_remote_copy(
-                src_ref=mine.at[at],
-                dst_ref=target.at[own],
-                send_sem=send_sem.at[6 + at],
-                recv_sem=recv_sem.at[6 + at],
-                device_id=peer_of(step),
-                device_id_type=MESH,
-            ).start()
+            send_to(peers_of(step))
             return carry
 
-        lax.fori_loop(0, count - 1, step_to, 0)
+        lax.fori_loop(0, 7, step_to, 0)
+        send_to(peers_of(7)[:-1])
         return pltpu.make_async_remote_copy(
             src_ref=target.at[pl.ds(0, count - 1)],
             dst_ref=target.at[pl.ds(0, count - 1)],
@@ -515,11 +535,11 @@
         )
 
     mine[0] = line
-    sent_a = spread(sum_a, peer_in_column, place, COLUMN, 0)
+    sent_a = spread(sum_a, peers_in_column, place, COLUMN, 0)
     wrapped = rows_inverse(flow) - start
     sent_a.wait_recv()
     mine[1] = jnp.sum(sum_a[...], axis=0)
-    sent_b = spread(sum_b, peer_in_plane, 8 * chip_x + chip_z, PLANE, 1)
+    sent_b = spread(sum_b, peers_in_plane, 8 * chip_x + chip_z, PLANE, 1)
     sent_b.wait_recv()
     line = jnp.sum(sum_b[...], axis=0) * (1.0 / (SEGS * GRID * GRID))
 
@@ -589,6 +609,7 @@
             pltpu.SemaphoreType.DMA((9,)),
             pltpu.SemaphoreType.DMA((9,)),
             pltpu.SemaphoreType.REGULAR,
+            pltpu.SemaphoreType.REGULAR,
         ],
         compiler_params=pltpu.CompilerParams(
             collective_id=0, has_side_effects=True, vmem_limit_bytes=54976 * 1024

time: 76.3 us -> 74 us (0.970)
  Pallas kernels: 73.1 us -> 70.7 us
    pallas_call x1, Pallas kernels: 73.1 us -> 70.7 us  [per_device(): pl.pallas_call(kernel, out_shape=(jax.ShapeDtypeStruct((1, ROWS, GRID), f...]
where the time goes in v5:
time: 74 us; the launch traced here: 73.8 us
  Pallas kernels  70.7 us (96%)
  local copies, waits for them, and re-layouts  1.82 us (2%)
  between operations  1.29 us (2%)
    pallas_call x1, Pallas kernels, per_device(): pl.pallas_call(kernel, out_shape=(jax.ShapeDtypeStruct((1, ROWS, GRID), f...  70.7 us

profile of v5, /device:TPU:1, one launch (start us, length us, event | category | flops | bytes accessed | tf_op | source)
XLA Modules:
  0.0 73.8 jit_solution(6983930312236975840)
XLA Ops:
  1.3 0.0 copy-start
  1.3 0.6 copy-done
  1.9 70.7 %shard_map.77 = (f32[1,32,1024]{2,1,0:T(8,128)S(1)}, f32[1,128]{1,0:T(1,128)S(1)}) custom-call(s32[1]{0:T(128)S(6)} %copy.9.steps_ref, s32[2]{0:T(128)S(1)} %copy-done, bf16[8,32,1024]{2,1,0:T(8,128)(2,1)} %bitcast.4, bf16[4,32,1024]{2,1,0:T(8,128)(2,1)} %bitcast.5, bf16[5248,256]{1,0:T(8,128)(2,1)} %constant.4.clone.table_hbm, ...), custom_call_target="tpu_custom_call" | custom-call | tf_op jit(solution)/shard_map/pallas_call | solution.py:586
  72.7 0.5 slice_bitcast_fusion
  73.2 0.7 copy.10
Async XLA Ops:
  1.3 0.7 copy-start

commit v6 on v5

--- a/solution.py
+++ b/solution.py
@@ -589,9 +589,12 @@
             jax.ShapeDtypeStruct((1, ROWS, GRID), f32),
             jax.ShapeDtypeStruct((1, 128), f32),
         ),
-        in_specs=[scalars, scalars] + [any_space] * 4,
-        out_specs=(pl.BlockSpec(memory_space=pltpu.VMEM),) * 2,
-        scratch_shapes=[
+        grid_spec=pltpu.PrefetchScalarGridSpec(
+            num_scalar_prefetch=2,
+            grid=(),
+            in_specs=[any_space] * 4,
+            out_specs=(pl.BlockSpec(memory_space=pltpu.VMEM),) * 2,
+            scratch_shapes=[
             pltpu.VMEM((KRYLOV, ROWS, GRID), bf16),
             pltpu.VMEM((4, ROWS, GRID), bf16),
             pltpu.VMEM(TABLE.shape, bf16),
@@ -611,6 +614,7 @@
             pltpu.SemaphoreType.REGULAR,
             pltpu.SemaphoreType.REGULAR,
         ],
+        ),
         compiler_params=pltpu.CompilerParams(
             collective_id=0, has_side_effects=True, vmem_limit_bytes=54976 * 1024
         ),

time: 74 us -> 73.5 us (level)
  no operation moved by 1% of the time
where the time goes in v6:
time: 73.5 us; the launch traced here: 73.3 us
  Pallas kernels  70.2 us (96%)
  local copies, waits for them, and re-layouts  1.82 us (2%)
  between operations  1.29 us (2%)
    pallas_call x1, Pallas kernels, per_device(): pl.pallas_call(kernel, out_shape=(jax.ShapeDtypeStruct((1, ROWS, GRID), f...  70.2 us

profile of v6, /device:TPU:1, one launch (start us, length us, event | category | flops | bytes accessed | tf_op | source)
XLA Modules:
  0.0 73.3 jit_solution(11082355903632030481)
XLA Ops:
  1.3 0.0 copy-start
  1.3 0.6 copy-done
  1.9 70.2 %shard_map.77 = (f32[1,32,1024]{2,1,0:T(8,128)S(1)}, f32[1,128]{1,0:T(1,128)S(1)}) custom-call(s32[1]{0:T(128)S(6)} %copy.9.steps_ref, s32[2]{0:T(128)S(1)} %copy-done, bf16[8,32,1024]{2,1,0:T(8,128)(2,1)} %bitcast.4, bf16[4,32,1024]{2,1,0:T(8,128)(2,1)} %bitcast.5, bf16[5248,256]{1,0:T(8,128)(2,1)} %constant.4.clone.table_hbm, ...), custom_call_target="tpu_custom_call" | custom-call | tf_op jit(solution)/shard_map/pallas_call | solution.py:586
  72.1 0.5 slice_bitcast_fusion
  72.7 0.7 copy.10
Async XLA Ops:
  1.3 0.7 copy-start

commit v7 on v6

--- a/solution.py
+++ b/solution.py
@@ -207,9 +207,9 @@
         pl.semaphore_signal(plane, inc=1, device_id=line_x(step), device_id_type=MESH)
         return carry
 
-    lax.fori_loop(0, SPACE // 4, greet_space, 0)
-    lax.fori_loop(0, 7, greet_z, 0)
-    lax.fori_loop(0, 3, greet_x, 0)
+    lax.fori_loop(0, SPACE // 4, greet_space, 0, unroll=True)
+    lax.fori_loop(0, 7, greet_z, 0, unroll=True)
+    lax.fori_loop(0, 3, greet_x, 0, unroll=True)
     for load in loads:
         load.start()
 

time: 73.5 us -> 73.5 us (level)
  no operation moved by 1% of the time
where the time goes in v7:
time: 73.5 us; the launch traced here: 73.3 us
  Pallas kernels  70.2 us (96%)
  local copies, waits for them, and re-layouts  1.82 us (2%)
  between operations  1.29 us (2%)
    pallas_call x1, Pallas kernels, per_device(): pl.pallas_call(kernel, out_shape=(jax.ShapeDtypeStruct((1, ROWS, GRID), f...  70.2 us

profile of v7, /device:TPU:1, one launch (start us, length us, event | category | flops | bytes accessed | tf_op | source)
XLA Modules:
  0.0 73.3 jit_solution(14143619440303439431)
XLA Ops:
  1.3 0.0 copy-start
  1.3 0.6 copy-done
  1.9 70.2 %shard_map.77 = (f32[1,32,1024]{2,1,0:T(8,128)S(1)}, f32[1,128]{1,0:T(1,128)S(1)}) custom-call(s32[1]{0:T(128)S(6)} %copy.9.steps_ref, s32[2]{0:T(128)S(1)} %copy-done, bf16[8,32,1024]{2,1,0:T(8,128)(2,1)} %bitcast.4, bf16[4,32,1024]{2,1,0:T(8,128)(2,1)} %bitcast.5, bf16[5248,256]{1,0:T(8,128)(2,1)} %constant.4.clone.table_hbm, ...), custom_call_target="tpu_custom_call" | custom-call | tf_op jit(solution)/shard_map/pallas_call | solution.py:586
  72.2 0.5 slice_bitcast_fusion
  72.7 0.7 copy.10
Async XLA Ops:
  1.3 0.7 copy-start
